TPU v7x, 128 devices: a whole 4x4x4 slice. The times are simulated.
128 devices in a mesh: row: 8 (over y, core), col: 16 (over x, z).
Axes of the slice: x: 4, y: 4, z: 4, core: 2. Of those that a mesh axis runs over, the one named last changes fastest.
Arguments:
- grad_out: bfloat16 [8, 16, 16, 16, 1024], P('row', 'col'), may hold values from -6 to 6
- block_in: bfloat16 [8, 16, 16, 16, 1024], P('row', 'col'), may hold values from -6 to 6
- mid: bfloat16 [8, 16, 16, 16, 1024], P('row', 'col'), may hold values from -6 to 6
- qkv: bfloat16 [8, 16, 16, 16, 3, 1024], P('row', 'col'), may hold values from -8 to 8
- gates: float32 [8, 16, 16, 16, 2], P('row', 'col'), may hold values from 0.05 to 1
- expert_ids: int32 [8, 16, 16, 16, 2], P('row', 'col'), may hold values from 0 to 31, all different within a row; in each aligned block of 256 rows (0 to 255, 256 to 511, ..., all dimensions but the last counted through in order) at most 32 rows name the same one
- w_in: bfloat16 [128, 1024, 1024], P(('row', 'col')), may hold values from -0.1875 to 0.1875
- w_out: bfloat16 [128, 1024, 1024], P(('row', 'col')), may hold values from -0.09375 to 0.09375
- w_qkv: bfloat16 [1024, 3072], replicated, may hold values from -0.1875 to 0.1875
- w_proj: bfloat16 [1024, 1024], replicated, may hold values from -0.1875 to 0.1875
- norm1: float32 [1024], replicated, may hold values from 0.5 to 1.5
- norm2: float32 [1024], replicated, may hold values from 0.5 to 1.5
Outputs:
- grad_in: bfloat16 [8, 16, 16, 16, 1024], P('row', 'col')
Inputs may be any that keep to these rules, and one draw needn't show every extreme that they name: `expert_ids`: among the 256 tokens of one device no expert is named more than 32 times, and in every draw some device names some expert exactly 32 times; the two experts of a token differ.
All inputs are finite; a program needn't handle non-finite values.
Results may differ from a plain program's by a relative error of at most 0.02.
Values may be sent and summed in bfloat16 or wider, within the bound.
A program may use at most 128 MiB of HBM per device.

v0:
```python
import jax
import jax.numpy as jnp
from jax import lax
from jax.sharding import PartitionSpec as P

HEADS = 32
E = 32
C = 32


EPSILON = 1e-05


def from_behind(block, axis, distance):
    devices = range(lax.axis_size(axis))
    route = [((i - distance) % len(devices), i) for i in devices]
    return lax.ppermute(block, axis, route)


def layer_stats(values):
    floats = values.astype(jnp.float32)
    centred = floats - jnp.mean(floats, -1, keepdims=True)
    inverse = lax.rsqrt(jnp.mean(centred * centred, -1, keepdims=True) + EPSILON)
    return (centred * inverse, inverse)


def norm_back(upstream, normal_hat, inverse, gain):
    scaled_up = upstream * gain
    first = jnp.mean(scaled_up, -1, keepdims=True)
    second = jnp.mean(scaled_up * normal_hat, -1, keepdims=True)
    return inverse * (scaled_up - first - normal_hat * second)


def gelu_slope(values):
    return (
        0.5 * (1.0 + lax.erf(values * 0.7071067811865476))
        + values * jnp.exp(-0.5 * values * values) * 0.3989422804014327
    )


def window_back(window_data, labels):
    tokens_in = window_data.shape[0]
    width = window_data.shape[2]
    head_size = width // HEADS
    scale = head_size ** (-0.5)
    parts = window_data.reshape(tokens_in, 4, HEADS, head_size)
    query = parts[:, 0]
    key_rows = parts[:, 1]
    value_rows = parts[:, 2]
    out_grad = parts[:, 3]
    scores = jnp.einsum("qhd,khd->hqk", query, key_rows, preferred_element_type=jnp.float32) * scale
    allowed = (labels[:, None] == labels[None, :])[None, :, :]
    highest = jnp.max(jnp.where(allowed, scores, -1e30), -1, keepdims=True)
    expo = jnp.exp(jnp.where(allowed, scores - highest, -1e30))
    probs = expo / jnp.sum(expo, -1, keepdims=True)
    probs_b = probs.astype(jnp.bfloat16)
    value_grad = jnp.einsum(
        "hqk,qhd->khd", probs_b, out_grad, preferred_element_type=jnp.float32
    ).astype(jnp.bfloat16)
    prob_grad = jnp.einsum("qhd,khd->hqk", out_grad, value_rows, preferred_element_type=jnp.float32)
    row_total = jnp.sum(probs * prob_grad, -1, keepdims=True)
    score_grad = (probs * (prob_grad - row_total)).astype(jnp.bfloat16)
    query_grad = (
        jnp.einsum("hqk,khd->qhd", score_grad, key_rows, preferred_element_type=jnp.float32) * scale
    ).astype(jnp.bfloat16)
    key_grad = (
        jnp.einsum("hqk,qhd->khd", score_grad, query, preferred_element_type=jnp.float32) * scale
    ).astype(jnp.bfloat16)
    return jnp.stack((query_grad, key_grad, value_grad), 1).reshape(tokens_in, 3, width)


def shards(
    grad_out, block_in, mid, qkv, gates, expert_ids, w_in, w_out, w_qkv, w_proj, norm1, norm2
):
    window = grad_out.shape[2]
    width = grad_out.shape[4]
    count = window * window
    half = window // 2
    owners = lax.axis_size(("row", "col"))
    group = owners // E
    grad_rows = grad_out.reshape(count, width)
    mid_hat, mid_inverse = layer_stats(mid.reshape(count, width))
    normed = (mid_hat * norm2).astype(jnp.bfloat16)
    sent_grad = (
        (gates.reshape(count, 2)[:, :, None] * grad_rows[:, None, :])
        .astype(jnp.bfloat16)
        .reshape(2 * count, width)
    )
    choices_flat = expert_ids.reshape(2 * count)
    expert_hot = (choices_flat[:, None] == jnp.arange(E, dtype=jnp.int32)[None, :]).astype(
        jnp.int32
    )
    slot_rank = jnp.sum((jnp.cumsum(expert_hot, 0) - 1) * expert_hot, 1)
    placed = choices_flat * C + slot_rank
    matched = placed[None, :] == jnp.arange(E * C, dtype=jnp.int32)[:, None]
    filled = jnp.any(matched, 1)
    pair_of = jnp.sum(jnp.where(matched, jnp.arange(2 * count, dtype=jnp.int32)[None, :], 0), 1)
    zero_value = jnp.zeros((), jnp.bfloat16)
    send_normed = jnp.where(filled[:, None], normed[pair_of // 2], zero_value)
    send_grad = jnp.where(filled[:, None], sent_grad[pair_of], zero_value)
    outgoing = jnp.stack((send_normed, send_grad), 1)
    spread_out = outgoing.reshape(E, 1, C, 2, width)
    spread_out = jnp.broadcast_to(spread_out, (E, group, C, 2, width)).reshape(owners, C, 2, width)
    first_proj = w_in[0]
    second_proj = w_out[0]
    arrived = lax.all_to_all(spread_out, ("row", "col"), split_axis=0, concat_axis=0, tiled=True)
    leading = arrived.shape[:2]
    normed_in = arrived[:, :, 0].reshape(-1, width)
    grad_part = arrived[:, :, 1].reshape(-1, width)
    pre = jnp.dot(normed_in, first_proj, preferred_element_type=jnp.float32)
    act_grad = jnp.einsum("rd,fd->rf", grad_part, second_proj, preferred_element_type=jnp.float32)
    pre_grad = (act_grad * gelu_slope(pre)).astype(jnp.bfloat16)
    shares = jnp.einsum(
        "rf,df->rd", pre_grad, first_proj, preferred_element_type=jnp.float32
    ).astype(jnp.bfloat16)
    returned = lax.all_to_all(
        shares.reshape(leading + (width,)), ("row", "col"), split_axis=0, concat_axis=0, tiled=True
    )
    summed = jnp.sum(returned.reshape(E, group, C, width).astype(jnp.float32), 1).reshape(
        E * C, width
    )
    normed_grad = jnp.sum(summed[placed].reshape(count, 2, width), 1)
    mid_grad = (
        grad_rows.astype(jnp.float32) + norm_back(normed_grad, mid_hat, mid_inverse, norm2)
    ).astype(jnp.bfloat16)
    context_grad = jnp.einsum(
        "td,ed->te", mid_grad, w_proj, preferred_element_type=jnp.float32
    ).astype(jnp.bfloat16)
    stacked = jnp.concatenate(
        (qkv.reshape(window, window, 3, width), context_grad.reshape(window, window, 1, width)), 2
    )
    right_part = from_behind(stacked[:, :half], "col", -1)
    widened = jnp.concatenate((stacked[:, half:], right_part), 1)
    lower_part = from_behind(widened[:half], "row", -1)
    shifted = jnp.concatenate((widened[half:], lower_part), 0)
    row_last = lax.axis_index("row") == lax.axis_size("row") - 1
    col_last = lax.axis_index("col") == lax.axis_size("col") - 1
    lower_half = jnp.arange(window) >= half
    row_label = (row_last & lower_half).astype(jnp.int32)
    col_label = (col_last & lower_half).astype(jnp.int32)
    labels = (row_label[:, None] * 2 + col_label[None, :]).reshape(count)
    window_grads = window_back(shifted.reshape(count, 4, width), labels).reshape(
        window, window, 3, width
    )
    from_above = from_behind(window_grads[half:], "row", 1)
    widened_grads = jnp.concatenate((from_above, window_grads[:half]), 0)
    from_left = from_behind(widened_grads[:, half:], "col", 1)
    qkv_grad = jnp.concatenate((from_left, widened_grads[:, :half]), 1).reshape(count, 3 * width)
    input_normed_grad = jnp.einsum("tc,dc->td", qkv_grad, w_qkv, preferred_element_type=jnp.float32)
    in_hat, in_inverse = layer_stats(block_in.reshape(count, width))
    result = mid_grad.astype(jnp.float32) + norm_back(input_normed_grad, in_hat, in_inverse, norm1)
    return result.astype(jnp.bfloat16).reshape(grad_out.shape)


def solution(mesh):
    return jax.shard_map(
        shards,
        mesh=mesh,
        in_specs=(
            P("row", "col", None, None, None),
            P("row", "col", None, None, None),
            P("row", "col", None, None, None),
            P("row", "col", None, None, None, None),
            P("row", "col", None, None, None),
            P("row", "col", None, None, None),
            P(("row", "col"), None, None),
            P(("row", "col"), None, None),
            P(),
            P(),
            P(),
            P(),
        ),
        out_specs=P("row", "col", None, None, None),
        check_vma=False,
    )
```

profile of v0, /device:TPU:1, one launch (start us, length us, event | category | flops | bytes accessed | tf_op | source)
XLA Modules:
  0.0 548.9 jit_solution(6951843319100312945)
XLA Ops:
  0.0 1.0 copy.56
  1.3 1.2 convert_reduce_fusion.1
  2.5 1.3 multiply_reduce_fusion.4
  3.9 1.2 reduce-window.6
  6.4 2.1 mul.210
  8.4 3.7 mul.211
  12.9 5.4 gather_fusion
  18.2 1.8 multiply_convert_fusion.1
  20.0 5.4 gather_fusion.1
  25.4 2.6 broadcast_select_fusion.1
  28.4 0.8 copy.60
  29.2 2.2 broadcast_in_dim.85
  31.4 200.6 %all_to_all.10 = bf16[128,32,2,1024]{3,1,2,0:T(8,128)(2,1)S(1)} all-to-all(bf16[128,32,2,1024]{3,1,2,0:T(8,128)(2,1)S(1)} %bitcast.156), channel_id=1, replica_groups=mesh['row'=8,'col'=16] {'row','col'}, dimensions={0} | all-to-all | bytes 33554432 | tf_op jit(solution)/shard_map/all_to_all | solution.py:106
  232.0 5.0 fusion.66
  237.0 11.7 %fusion.17 = f32[4096,1024]{1,0:T(8,128)} fusion(bf16[4096,1024]{1,0:T(8,128)(2,1)S(1)} %bitcast.165, bf16[1,1024,1024]{2,1,0:T(8,128)(2,1)S(1)} %copy-done), kind=kOutput, calls=%fused_computation.32 | convolution fusion | flops 8589934592 | bytes 27262976 | tf_op jit(solution)/shard_map/dot_general | solution.py:110
  248.7 27.7 %convolution_convert_fusion = bf16[4096,1024]{1,0:T(8,128)(2,1)} fusion(f32[4096,1024]{1,0:T(8,128)} %fusion.17, bf16[4096,1024]{1,0:T(8,128)(2,1)} %bitcast.164, bf16[1,1024,1024]{2,1,0:T(8,128)(2,1)S(1)} %copy-done, bf16[1,1024,1024]{2,1,0:T(8,128)(2,1)} %param.19), kind=kOutput, calls=%fused_computation.17 | convolution fusion | flops 17226006528 | bytes 37748736 | tf_op jit(solution)/shard_map/rf,df->rd/dot_general | solution.py:113
  276.5 6.8 %all-to-all-start.1 = ((bf16[128,32,1024]{2,1,0:T(8,128)(2,1)}), bf16[128,32,1024]{2,1,0:T(8,128)(2,1)}, u32[]{:S(2)}, u32[]{:S(2)}) async-start(bf16[128,32,1024]{2,1,0:T(8,128)(2,1)} %bitcast.161), calls=%async_computation.1 | async-start | bytes 16777216 | tf_op jit(solution)/shard_map/all_to_all | solution.py:116
  283.7 99.7 %all-to-all-done.1 = bf16[128,32,1024]{2,1,0:T(8,128)(2,1)} async-done(((bf16[128,32,1024]{2,1,0:T(8,128)(2,1)}), bf16[128,32,1024]{2,1,0:T(8,128)(2,1)}, u32[]{:S(2)}, u32[]{:S(2)}) %all-to-all-start.1) | async-done | bytes 8388640 | tf_op jit(solution)/shard_map/all_to_all | solution.py:116
  383.4 8.0 %convert_reduce_fusion = f32[32,32,1024]{2,1,0:T(8,128)} fusion(bf16[128,32,1024]{2,1,0:T(8,128)(2,1)} %all-to-all-done.1), kind=kLoop, calls=%fused_computation.11 | loop fusion | flops 7340032 | bytes 12582912 | tf_op jit(solution)/shard_map/reduce_sum | solution.py:119
  391.4 5.0 gather_fusion.2
  396.4 2.3 reshape.412
  398.7 4.1 reduce_sum.139
  406.9 7.5 %collective-permute-start = (bf16[16,8,4,1024]{3,1,2,0:T(8,128)(2,1)S(1)}, bf16[16,8,4,1024]{3,1,2,0:T(8,128)(2,1)S(1)}, u32[]{:S(2)}, u32[]{:S(2)}) collective-permute-start(bf16[16,8,4,1024]{3,1,2,0:T(8,128)(2,1)S(1)} %get-tuple-element.16), channel_id=1, source_target_pairs={{1,0},{2,1},{3,2},{4,3},{5,4},{6,5},{7,6},{8,7},{9,8},{10,9},{11,1... | collective-permute-start | bytes 3145736 | tf_op jit(solution)/shard_map/ppermute | solution.py:17
  414.5 21.9 %collective-permute-done = bf16[16,8,4,1024]{3,1,2,0:T(8,128)(2,1)S(1)} collective-permute-done((bf16[16,8,4,1024]{3,1,2,0:T(8,128)(2,1)S(1)}, bf16[16,8,4,1024]{3,1,2,0:T(8,128)(2,1)S(1)}, u32[]{:S(2)}, u32[]{:S(2)}) %collective-permute-start) | collective-permute-done | bytes 1048608 | tf_op jit(solution)/shard_map/ppermute | solution.py:17
  436.9 13.9 %collective-permute-done.1 = bf16[8,16,4,1024]{3,1,2,0:T(8,128)(2,1)S(1)} collective-permute-done((bf16[8,16,4,1024]{3,1,2,0:T(8,128)(2,1)S(1)}, bf16[8,16,4,1024]{3,1,2,0:T(8,128)(2,1)S(1)}, u32[]{:S(2)}, u32[]{:S(2)}) %collective-permute-start.1) | collective-permute-done | bytes 1048608 | tf_op jit(solution)/shard_map/ppermute | solution.py:17
  451.2 7.9 %reshape_reshape.4 = bf16[256,4,32,32]{3,2,0,1:T(8,128)(2,1)} reshape(bf16[16,16,4,1024]{3,1,0,2:T(8,128)(2,1)S(1)} %copy.65) | data formatting | bytes 4194304 | tf_op jit(solution)/shard_map/reshape;reshape | solution.py:46
  459.1 5.8 %fusion.67 = (bf16[256,1,32,32]{3,2,0,1:T(8,128)(2,1)S(1)}, bf16[256,1,32,32]{3,2,0,1:T(8,128)(2,1)}, bf16[256,1,32,32]{3,2,0,1:T(8,128)(2,1)}, bf16[256,1,32,32]{3,2,0,1:T(8,128)(2,1)}) fusion(bf16[256,4,32,32]{3,2,0,1:T(8,128)(2,1)} %reshape_reshape.4), kind=kLoop, calls=%fused_computation.127 | loop fusion | bytes 4194304 | tf_op jit(solution)/shard_map/slice | solution.py:49
  464.9 2.8 copy.81
  467.6 2.8 copy.82
  470.4 3.4 copy.83
  473.9 2.4 copy.84
  476.2 5.7 %fusion.70 = (f32[32,256]{1,0:T(8,128)S(1)}, f32[32,256,256]{1,2,0:T(8,128)}) fusion(pred[256,256]{0,1:T(8,128)(4,1)S(1)} %broadcast_compare_fusion, bf16[256,1,32,32]{0,3,2,1:T(8,128)(2,1)S(1)} %copy.82, bf16[256,1,32,32]{0,3,2,1:T(8,128)(2,1)S(1)} %copy.81), kind=kOutput, calls=%fused_computation.130 | convolution fusion | flops 281018624 | bytes 9535488 | tf_op jit(solution)/shard_map/sub | solution.py:54
  481.9 4.9 multiply_reduce_fusion
  486.9 0.9 slice-done.1
  487.8 1.8 multiply_convert_fusion
  490.4 1.3 fusion.27
  491.7 1.4 fusion.29
  493.3 1.2 fusion.69
  494.4 6.0 %copy.73 = bf16[128,3,32,32]{3,2,0,1:T(8,128)(2,1)} copy(bf16[128,3,32,32]{0,3,2,1:T(8,128)(2,1)} %get-tuple-element.20) | data formatting | bytes 1572864 | tf_op jit(solution)/shard_map/slice | solution.py:145
  500.5 4.8 slice.67
  505.3 5.0 copy.74
  510.3 4.8 slice.69
  515.2 1.2 constant_dynamic-update-slice_fusion.1
  516.5 1.0 fusion.68
  518.1 22.1 %collective-permute-done.3 = bf16[16,8,3,1024]{3,1,0,2:T(8,128)(2,1)S(1)} collective-permute-done((bf16[16,8,3,1024]{3,1,0,2:T(8,128)(2,1)}, bf16[16,8,3,1024]{3,1,0,2:T(8,128)(2,1)S(1)}, u32[]{:S(2)}, u32[]{:S(2)}) %collective-permute-start.3) | collective-permute-done | bytes 786464 | tf_op jit(solution)/shard_map/ppermute | solution.py:17
  540.3 1.4 copy.75
  542.5 4.9 fusion.65
  547.5 1.2 add_convert_fusion
  (98 shorter events, 10.5 us)
Async XLA Ops:
  0.0 237.0 %copy-start = (bf16[1,1024,1024]{2,1,0:T(8,128)(2,1)S(1)}, bf16[1,1024,1024]{2,1,0:T(8,128)(2,1)}, u32[]{:S(2)}) copy-start(bf16[1,1024,1024]{2,1,0:T(8,128)(2,1)} %param.18) | copy-start | bytes 6291460
  0.0 6.2 %copy-start.5 = (bf16[1,1,16,16,1024]{4,3,2,1,0:T(8,128)(2,1)S(1)}, bf16[1,1,16,16,1024]{4,3,2,1,0:T(8,128)(2,1)}, u32[]{:S(2)}) copy-start(bf16[1,1,16,16,1024]{4,3,2,1,0:T(8,128)(2,1)} %param.12) | copy-start | bytes 1572868
  8.4 3.7 copy-start.14
  8.4 4.1 copy-start.2
  8.4 4.1 copy-start.12
  276.5 6.9 %copy-start.13 = (s32[1,1,16,16,2]{3,4,2,1,0:T(2,128)S(1)}, s32[1,1,16,16,2]{3,4,2,1,0:T(2,128)}, u32[]{:S(2)}) copy-start(s32[1,1,16,16,2]{3,4,2,1,0:T(2,128)} %param.17) | copy-start | bytes 6148
  276.5 107.0 %all-to-all-start.1 = ((bf16[128,32,1024]{2,1,0:T(8,128)(2,1)}), bf16[128,32,1024]{2,1,0:T(8,128)(2,1)}, u32[]{:S(2)}, u32[]{:S(2)}) async-start(bf16[128,32,1024]{2,1,0:T(8,128)(2,1)} %bitcast.161), calls=%async_computation.1 | async-start | bytes 16777216 | tf_op jit(solution)/shard_map/all_to_all | solution.py:116
  398.7 4.3 copy-start.3
  402.9 1.0 copy-start.6
  403.5 1.6 copy-start.15
  405.1 0.8 copy-start.7
  405.1 1.6 copy-start.9
  406.9 29.4 %collective-permute-start = (bf16[16,8,4,1024]{3,1,2,0:T(8,128)(2,1)S(1)}, bf16[16,8,4,1024]{3,1,2,0:T(8,128)(2,1)S(1)}, u32[]{:S(2)}, u32[]{:S(2)}) collective-permute-start(bf16[16,8,4,1024]{3,1,2,0:T(8,128)(2,1)S(1)} %get-tuple-element.16), channel_id=1, source_target_pairs={{1,0},{2,1},{3,2},{4,3},{5,4},{6,5},{7,6},{8,7},{9,8},{10,9},{11,1... | collective-permute-start | bytes 3145736 | tf_op jit(solution)/shard_map/ppermute | solution.py:17
  436.6 14.2 %collective-permute-start.1 = (bf16[8,16,4,1024]{3,1,2,0:T(8,128)(2,1)S(1)}, bf16[8,16,4,1024]{3,1,2,0:T(8,128)(2,1)S(1)}, u32[]{:S(2)}, u32[]{:S(2)}) collective-permute-start(bf16[8,16,4,1024]{3,1,2,0:T(8,128)(2,1)S(1)} %get-tuple-element.14), channel_id=1, source_target_pairs={{16,0},{32,16},{48,32},{64,48},{80,64},{96,80},{112,96},{0,112},{1... | collective-permute-start | bytes 3145736 | tf_op jit(solution)/shard_map/ppermute | solution.py:17
  476.2 5.7 %copy-start.10 = (bf16[256,1,32,32]{0,3,2,1:T(8,128)(2,1)S(1)}, bf16[256,1,32,32]{0,3,2,1:T(8,128)(2,1)}, u32[]{:S(2)}) copy-start(bf16[256,1,32,32]{0,3,2,1:T(8,128)(2,1)} %copy.83) | copy-start | bytes 1572868
  476.2 5.7 %copy-start.11 = (bf16[256,1,32,32]{0,3,2,1:T(8,128)(2,1)S(1)}, bf16[256,1,32,32]{0,3,2,1:T(8,128)(2,1)}, u32[]{:S(2)}) copy-start(bf16[256,1,32,32]{0,3,2,1:T(8,128)(2,1)} %copy.84) | copy-start | bytes 1572868
  481.9 4.9 slice-start
  481.9 5.8 %slice-start.1 = ((s8[8388608]{0:T(1024)(128)(4,1)}), s8[4194304]{0:T(1024)(128)(4,1)S(1)}, s32[]{:S(2)}) async-start(s8[8388608]{0:T(1024)(128)(4,1)} %bitcast.159), calls=%async_computation.3 | async-start | bytes 8388608
  505.3 9.9 %collective-permute-start.2 = (bf16[8,16,3,1024]{3,1,0,2:T(8,128)(2,1)S(1)}, bf16[8,16,3,1024]{3,1,0,2:T(8,128)(2,1)}, u32[]{:S(2)}, u32[]{:S(2)}) collective-permute-start(bf16[8,16,3,1024]{3,1,0,2:T(8,128)(2,1)S(1)} %slice.67), channel_id=1, source_target_pairs={{112,0},{0,16},{16,32},{32,48},{48,64},{64,80},{80,96},{96,112},{1... | collective-permute-start | bytes 2359304 | tf_op jit(solution)/shard_map/ppermute | solution.py:17
  516.4 1.1 copy-start.4
  517.5 22.7 %collective-permute-start.3 = (bf16[16,8,3,1024]{3,1,0,2:T(8,128)(2,1)}, bf16[16,8,3,1024]{3,1,0,2:T(8,128)(2,1)S(1)}, u32[]{:S(2)}, u32[]{:S(2)}) collective-permute-start(bf16[16,8,3,1024]{3,1,0,2:T(8,128)(2,1)} %get-tuple-element.17), channel_id=1, source_target_pairs={{15,0},{0,1},{1,2},{2,3},{3,4},{4,5},{5,6},{6,7},{7,8},{8,9},{9,10... | collective-permute-start | bytes 2359304 | tf_op jit(solution)/shard_map/ppermute | solution.py:17
  541.7 0.8 copy-start.16
  542.5 5.0 copy-start.8
  542.5 6.2 %copy-start.1 = (bf16[1,1024,1024]{2,1,0:T(8,128)(2,1)S(1)}, bf16[1,1024,1024]{2,1,0:T(8,128)(2,1)}, u32[]{:S(2)}) copy-start(bf16[1,1024,1024]{2,1,0:T(8,128)(2,1)} %param.18) | copy-start | bytes 6291460
where the time goes:
time: 555 us; the launch traced here: 549 us
  blocking collectives  201 us (36%)
  waiting for transfers between devices  158 us (28%)
  local copies, waits for them, and re-layouts  89 us (16%)
  matrix products  59.3 us (11%)
  other arithmetic  27.2 us (5%)
  starting transfers between devices  14.4 us (3%)
    all_to_all x1, blocking collectives, shards(): lax.all_to_all(spread_out, ('row', 'col'), split_axis=0, concat_axis=0, t...  201 us
    all_to_all x1, waiting for transfers between devices, shards(): lax.all_to_all(shares.reshape(leading + (width,)), ('row', 'col'), split_...  99.7 us
    ppermute x4, waiting for transfers between devices, from_behind(): return lax.ppermute(block, axis, route)  57.8 us
    dot_general x1, matrix products, shards(): jnp.einsum('rf,df->rd', pre_grad, first_proj, preferred_element_type=jnp....  27.7 us
    unnamed x46, local copies, waits for them, and re-layouts  17.4 us
    dot_general x1, matrix products, shards(): pre = jnp.dot(normed_in, first_proj, preferred_element_type=jnp.float32)  11.7 us
  transfers between devices with their start and end apart: 5, of which 4 were waited for; matrix products, arithmetic and copies ran while one was open for 2% of the time, Pallas kernels for 0%

commit v1 on v0

v1 whole, which is shorter than its diff:
```python
import jax
import jax.numpy as jnp
from jax import lax
from jax.experimental import pallas as pl
from jax.experimental.pallas import tpu as pltpu
from jax.sharding import PartitionSpec as P

HEADS = 32
E = 32
C = 32
EPSILON = 1e-05
MESH = pl.DeviceIdType.MESH
F32 = jnp.float32
BF16 = jnp.bfloat16
HID = 512
PIECES = 8


def from_behind(block, axis, distance):
    devices = range(lax.axis_size(axis))
    route = [((i - distance) % len(devices), i) for i in devices]
    return lax.ppermute(block, axis, route)


def layer_stats(values):
    floats = values.astype(F32)
    centred = floats - jnp.mean(floats, -1, keepdims=True)
    inverse = lax.rsqrt(jnp.mean(centred * centred, -1, keepdims=True) + EPSILON)
    return (centred * inverse, inverse)


def norm_back(upstream, normal_hat, inverse, gain):
    scaled_up = upstream * gain
    first = jnp.mean(scaled_up, -1, keepdims=True)
    second = jnp.mean(scaled_up * normal_hat, -1, keepdims=True)
    return inverse * (scaled_up - first - normal_hat * second)


def gelu_slope(values):
    return (
        0.5 * (1.0 + lax.erf(values * 0.7071067811865476))
        + values * jnp.exp(-0.5 * values * values) * 0.3989422804014327
    )


def dot(a, b, contract=(1, 0)):
    return lax.dot_general(
        a, b, (((contract[0],), (contract[1],)), ((), ())), preferred_element_type=F32
    )


def to_quadrants(x):
    n = x.shape[-1]
    parts = x.reshape(2, 8, 2, 8, n)
    return jnp.concatenate(
        [parts[a, :, b].reshape(64, n) for a in range(2) for b in range(2)], 0
    )


def from_quadrants(x):
    n = x.shape[-1]
    parts = x.reshape(2, 2, 8, 8, n)
    rows = []
    for a in range(2):
        for i in range(8):
            rows.append(jnp.concatenate([parts[a, 0, i], parts[a, 1, i]], 0))
    return jnp.concatenate(rows, 0)


def position():
    row, col = lax.axis_index("row"), lax.axis_index("col")
    return lax.div(col, 4), lax.div(row, 2), lax.rem(row, 2), lax.rem(col, 4)


def place(x, y, c, z):
    return (2 * y + c, 4 * x + z)


def moe_kernel(
    mid_ref,
    grad_ref,
    gates_ref,
    ids_ref,
    w_in_ref,
    w_out_ref,
    norm2_ref,
    out_ref,
    w_first,
    w_second,
    outgoing,
    arrived,
    total,
    ret_out,
    ret_in,
    choice,
    w_send,
    w_recv,
    d_send,
    d_recv,
    r_send,
    r_recv,
):
    x, y, c, z = position()
    pair = lax.div(z, 2)
    u = z + 1 - 2 * lax.rem(z, 2)
    w = 3 - z
    v = 3 - u
    other = 1 - c
    twin = place(x, y, other, z)
    me = 8 * y + 4 * pair + x

    def member(e):
        ex, ey, eb = lax.rem(e, 4), lax.div(e, 8), lax.rem(lax.div(e, 4), 2)
        differs = lax.rem(eb + pair, 2)
        return place(ex, ey, c, z + differs * (3 - 2 * z))

    barrier = pltpu.get_barrier_semaphore()

    def greet(e, carry):
        @pl.when(e != me)
        def _():
            pl.semaphore_signal(barrier, inc=1, device_id=member(e), device_id_type=MESH)

        return carry

    lax.fori_loop(0, E, greet, 0)
    for where in (twin, place(x, y, 0, u), place(x, y, 1, u), place(x, y, other, w)):
        pl.semaphore_signal(barrier, inc=1, device_id=where, device_id_type=MESH)
    pl.semaphore_wait(barrier, E - 1 + 4)

    def source(which, h):
        if which == 0:
            return w_in_ref.at[:, pl.ds(h * HID, HID)]
        return w_out_ref.at[pl.ds(h * HID, HID), :]

    store = (w_first, w_second)

    def ship(which, src, piece, send_at, where):
        return pltpu.make_async_remote_copy(
            src_ref=src,
            dst_ref=store[which].at[piece],
            send_sem=w_send.at[which, send_at],
            recv_sem=w_recv.at[which, piece],
            device_id=where,
            device_id_type=MESH,
        )

    def local(which, h):
        piece = 2 * z + h
        return pltpu.make_async_copy(
            source(which, h), store[which].at[piece], w_recv.at[which, piece]
        )

    inside = c == pair

    @pl.when(inside)
    def _():
        for h in range(2):
            for which in range(2):
                ship(which, source(which, h), 2 * z + h, h, place(x, y, h, u)).start()
        for h in range(2):
            for which in range(2):
                ship(which, source(which, h), 2 * z + h, 2 + h, twin).start()
                local(which, h).start()

    @pl.when(jnp.logical_not(inside))
    def _():
        for h in range(2):
            for which in range(2):
                ship(which, source(which, h), 2 * z + h, h, place(x, y, h, w)).start()

    norm2 = norm2_ref[...]
    grad = to_quadrants(grad_ref[...].astype(F32))
    mid_hat, mid_inverse = layer_stats(to_quadrants(mid_ref[...].astype(F32)))
    normed = (mid_hat * norm2).astype(BF16)
    gates = gates_ref[...]
    ids = ids_ref[...]
    sent = [(gates[:, k : k + 1] * grad).astype(BF16) for k in range(2)]
    lanes = lax.broadcasted_iota(jnp.int32, (256, E), 1)
    hots = [ids[:, k : k + 1] == lanes for k in range(2)]
    before = (
        lax.broadcasted_iota(jnp.int32, (256, 256), 0)
        > lax.broadcasted_iota(jnp.int32, (256, 256), 1)
    ).astype(BF16)
    hot_f = [h.astype(F32) for h in hots]
    ranks = [dot(before, h.astype(BF16)) for h in hot_f]
    ranks[1] = ranks[1] + jnp.sum(hot_f[0], 0, keepdims=True)
    slots = [
        ids[:, k : k + 1] * C
        + jnp.sum(hot_f[k] * ranks[k], 1, keepdims=True).astype(jnp.int32)
        for k in range(2)
    ]
    wide = lax.broadcasted_iota(jnp.int32, (256, E * C), 1)
    choice[...] = ((slots[0] == wide) | (slots[1] == wide)).astype(BF16)

    def ship_rows(e):
        return pltpu.make_async_remote_copy(
            src_ref=outgoing.at[e],
            dst_ref=arrived.at[me],
            send_sem=d_send.at[e],
            recv_sem=d_recv.at[me],
            device_id=member(e),
            device_id_type=MESH,
        )

    def keep_rows():
        return pltpu.make_async_copy(outgoing.at[me], arrived.at[me], d_recv.at[me])

    narrow = lax.broadcasted_iota(jnp.int32, (256, 256), 1)

    def dispatch(step, carry):
        block = lax.rem(y + step, 4)
        base = block * 256
        picks = [(slots[k] == narrow + base).astype(BF16) for k in range(2)]
        rows_n = dot(picks[0] + picks[1], normed, (0, 0))
        rows_g = dot(picks[0], sent[0], (0, 0)) + dot(picks[1], sent[1], (0, 0))
        outgoing[pl.ds(block * 8, 8), 0] = rows_n.astype(BF16).reshape(8, C, 1024)
        outgoing[pl.ds(block * 8, 8), 1] = rows_g.astype(BF16).reshape(8, C, 1024)

        def send_one(k, carry):
            e = block * 8 + lax.rem(4 * pair + x + k, 8)

            @pl.when(e != me)
            def _():
                ship_rows(e).start()

            @pl.when(e == me)
            def _():
                keep_rows().start()

            return carry

        return lax.fori_loop(0, 8, send_one, carry)

    lax.fori_loop(0, 4, dispatch, 0)
    total[...] = jnp.zeros_like(total)

    def landed(which, piece):
        pltpu.make_async_copy(
            store[which].at[piece], store[which].at[piece], w_recv.at[which, piece]
        ).wait()

    def pass_on(piece, send_at, targets):
        for which in range(2):
            landed(which, piece)
            for n, where in enumerate(targets):
                ship(which, store[which].at[piece], piece, send_at + n, where).start()

    def product(piece, rows, begin):
        count = rows // C
        at = pl.ds(begin, count)
        normed_rows = arrived[at, 0].reshape(rows, 1024)
        grad_rows = arrived[at, 1].reshape(rows, 1024)
        first, second = w_first[piece], w_second[piece]
        pre = dot(normed_rows, first)
        act_grad = dot(grad_rows, second, (1, 1))
        pre_grad = (act_grad * gelu_slope(pre)).astype(BF16)
        return dot(pre_grad, first, (1, 1))

    def whole(piece, rows=512):
        def one(step, carry):
            at = pl.ds(pl.multiple_of(step * rows, rows), rows)
            total[at] = total[at] + product(piece, rows, step * (rows // C))
            return carry

        lax.fori_loop(0, 1024 // rows, one, 0)

    pass_on(2 * w + c, 4, (place(x, y, c, u), twin))
    pass_on(2 * u + c, 6, (twin,))

    def rows_landed(m, carry):
        pltpu.make_async_copy(arrived.at[m], arrived.at[m], d_recv.at[m]).wait()
        return carry

    lax.fori_loop(0, E, rows_landed, 0)
    for h in range(2):
        for which in range(2):
            landed(which, 2 * z + h)
        whole(2 * z + h)
    whole(2 * u + c)
    whole(2 * w + c)
    for which in range(2):
        landed(which, 2 * u + other)
    whole(2 * u + other)
    for which in range(2):
        landed(which, 2 * w + other)
    whole(2 * w + other)
    pass_on(2 * v + c, 7, (twin,))
    whole(2 * v + c)
    for which in range(2):
        landed(which, 2 * v + other)

    def ship_back(m):
        return pltpu.make_async_remote_copy(
            src_ref=ret_out.at[m],
            dst_ref=ret_in.at[me],
            send_sem=r_send.at[m],
            recv_sem=r_recv.at[me],
            device_id=member(m),
            device_id_type=MESH,
        )

    def last(step, carry):
        block = lax.rem(y + step, 4)
        at = pl.ds(pl.multiple_of(block * 256, 256), 256)
        done = total[at] + product(2 * v + other, 256, block * 8)
        ret_out[pl.ds(block * 8, 8)] = done.astype(BF16).reshape(8, C, 1024)

        def send_one(k, carry):
            m = block * 8 + lax.rem(4 * pair + x + k, 8)

            @pl.when(m != me)
            def _():
                ship_back(m).start()

            @pl.when(m == me)
            def _():
                pltpu.make_async_copy(
                    ret_out.at[me], ret_in.at[me], r_recv.at[me]
                ).start()

            return carry

        return lax.fori_loop(0, 8, send_one, carry)

    lax.fori_loop(0, 4, last, 0)

    def back_landed(m, carry):
        pltpu.make_async_copy(ret_in.at[m], ret_in.at[m], r_recv.at[m]).wait()
        return carry

    lax.fori_loop(0, E, back_landed, 0)
    normed_grad = dot(choice[...], ret_in[...].reshape(E * C, 1024))
    mid_grad = grad + norm_back(normed_grad, mid_hat, mid_inverse, norm2)
    out_ref[...] = from_quadrants(mid_grad).astype(BF16)

    def sent_all(e, carry):
        @pl.when(e != me)
        def _():
            ship_rows(e).wait_send()
            ship_back(e).wait_send()

        return carry

    lax.fori_loop(0, E, sent_all, 0)

    def left(which, send_at):
        ship(which, store[which].at[0], 0, send_at, twin).wait_send()

    for which in range(2):
        for send_at in (0, 1, 4, 5, 6, 7):
            left(which, send_at)

    @pl.when(inside)
    def _():
        for which in range(2):
            for send_at in (2, 3):
                left(which, send_at)


def moe(mid, grad, gates, ids, w_in, w_out, norm2):
    vmem = pl.BlockSpec(memory_space=pltpu.VMEM)
    anywhere = pl.BlockSpec(memory_space=pl.ANY)
    dma = pltpu.SemaphoreType.DMA
    return pl.pallas_call(
        moe_kernel,
        out_shape=jax.ShapeDtypeStruct((256, 1024), BF16),
        in_specs=[vmem, vmem, vmem, vmem, anywhere, anywhere, vmem],
        out_specs=vmem,
        scratch_shapes=[
            pltpu.VMEM((PIECES, 1024, HID), BF16),
            pltpu.VMEM((PIECES, HID, 1024), BF16),
            pltpu.VMEM((E, 2, C, 1024), BF16),
            pltpu.VMEM((E, 2, C, 1024), BF16),
            pltpu.VMEM((E * C, 1024), F32),
            pltpu.VMEM((E, C, 1024), BF16),
            pltpu.VMEM((E, C, 1024), BF16),
            pltpu.VMEM((256, E * C), BF16),
            dma((2, 8)),
            dma((2, 8)),
            dma((E,)),
            dma((E,)),
            dma((E,)),
            dma((E,)),
        ],
        compiler_params=pltpu.CompilerParams(
            collective_id=0, has_side_effects=True, vmem_limit_bytes=60 * 1024 * 1024
        ),
        name="moe",
    )(mid, grad, gates, ids, w_in, w_out, norm2)


def window_back(window_data, labels):
    tokens_in = window_data.shape[0]
    width = window_data.shape[2]
    head_size = width // HEADS
    scale = head_size ** (-0.5)
    parts = window_data.reshape(tokens_in, 4, HEADS, head_size)
    query = parts[:, 0]
    key_rows = parts[:, 1]
    value_rows = parts[:, 2]
    out_grad = parts[:, 3]
    scores = jnp.einsum("qhd,khd->hqk", query, key_rows, preferred_element_type=F32) * scale
    allowed = (labels[:, None] == labels[None, :])[None, :, :]
    highest = jnp.max(jnp.where(allowed, scores, -1e30), -1, keepdims=True)
    expo = jnp.exp(jnp.where(allowed, scores - highest, -1e30))
    probs = expo / jnp.sum(expo, -1, keepdims=True)
    probs_b = probs.astype(BF16)
    value_grad = jnp.einsum(
        "hqk,qhd->khd", probs_b, out_grad, preferred_element_type=F32
    ).astype(BF16)
    prob_grad = jnp.einsum("qhd,khd->hqk", out_grad, value_rows, preferred_element_type=F32)
    row_total = jnp.sum(probs * prob_grad, -1, keepdims=True)
    score_grad = (probs * (prob_grad - row_total)).astype(BF16)
    query_grad = (
        jnp.einsum("hqk,khd->qhd", score_grad, key_rows, preferred_element_type=F32) * scale
    ).astype(BF16)
    key_grad = (
        jnp.einsum("hqk,qhd->khd", score_grad, query, preferred_element_type=F32) * scale
    ).astype(BF16)
    return jnp.stack((query_grad, key_grad, value_grad), 1).reshape(tokens_in, 3, width)


def shards(
    grad_out, block_in, mid, qkv, gates, expert_ids, w_in, w_out, w_qkv, w_proj, norm1, norm2
):
    window = grad_out.shape[2]
    width = grad_out.shape[4]
    count = window * window
    half = window // 2

    def columns(a):
        return a.reshape(2, half, 2, half, 2).transpose(0, 2, 1, 3, 4).reshape(count, 2)

    mid_grad = moe(
        mid.reshape(count, width),
        grad_out.reshape(count, width),
        columns(gates),
        columns(expert_ids),
        w_in[0],
        w_out[0],
        norm2.reshape(1, width),
    )
    context_grad = jnp.einsum("td,ed->te", mid_grad, w_proj, preferred_element_type=F32).astype(
        BF16
    )
    stacked = jnp.concatenate(
        (qkv.reshape(window, window, 3, width), context_grad.reshape(window, window, 1, width)), 2
    )
    right_part = from_behind(stacked[:, :half], "col", -1)
    widened = jnp.concatenate((stacked[:, half:], right_part), 1)
    lower_part = from_behind(widened[:half], "row", -1)
    shifted = jnp.concatenate((widened[half:], lower_part), 0)
    row_last = lax.axis_index("row") == lax.axis_size("row") - 1
    col_last = lax.axis_index("col") == lax.axis_size("col") - 1
    lower_half = jnp.arange(window) >= half
    row_label = (row_last & lower_half).astype(jnp.int32)
    col_label = (col_last & lower_half).astype(jnp.int32)
    labels = (row_label[:, None] * 2 + col_label[None, :]).reshape(count)
    window_grads = window_back(shifted.reshape(count, 4, width), labels)
    window_grads = jnp.einsum(
        "tc,dc->td", window_grads.reshape(count, 3 * width), w_qkv, preferred_element_type=F32
    )
    window_grads = window_grads.astype(BF16).reshape(window, window, width)
    from_above = from_behind(window_grads[half:], "row", 1)
    widened_grads = jnp.concatenate((from_above, window_grads[:half]), 0)
    from_left = from_behind(widened_grads[:, half:], "col", 1)
    input_normed_grad = jnp.concatenate((from_left, widened_grads[:, :half]), 1)
    input_normed_grad = input_normed_grad.reshape(count, width).astype(F32)
    in_hat, in_inverse = layer_stats(block_in.reshape(count, width))
    result = mid_grad.astype(F32) + norm_back(input_normed_grad, in_hat, in_inverse, norm1)
    return result.astype(BF16).reshape(grad_out.shape)


def solution(mesh):
    return jax.shard_map(
        shards,
        mesh=mesh,
        in_specs=(
            P("row", "col", None, None, None),
            P("row", "col", None, None, None),
            P("row", "col", None, None, None),
            P("row", "col", None, None, None, None),
            P("row", "col", None, None, None),
            P("row", "col", None, None, None),
            P(("row", "col"), None, None),
            P(("row", "col"), None, None),
            P(),
            P(),
            P(),
            P(),
        ),
        out_specs=P("row", "col", None, None, None),
        check_vma=False,
    )
```

time: 555 us -> 279 us (0.50)
  blocking collectives: 201 us -> 0 us
  Pallas kernels: 0 us -> 168 us
  waiting for transfers between devices: 158 us -> 46.9 us
  local copies, waits for them, and re-layouts: 89 us -> 30.4 us
  matrix products: 59.3 us -> 17.8 us
  other arithmetic: 27.2 us -> 6.9 us
  starting transfers between devices: 14.4 us -> 3.76 us
    all_to_all x1 -> x0, blocking collectives: 201 us -> none  [shards(): lax.all_to_all(spread_out, ('row', 'col'), split_axis=0, concat_axis=0, t...]
    pallas_call x0 -> x1, Pallas kernels: none -> 168 us  [moe(): pl.pallas_call(moe_kernel, out_shape=jax.ShapeDtypeStruct((256, 1024), BF...]
    all_to_all x1 -> x0, waiting for transfers between devices: 99.7 us -> none  [shards(): lax.all_to_all(shares.reshape(leading + (width,)), ('row', 'col'), split_...]
    dot_general x8 -> x6, matrix products: 53.6 us -> 12.1 us  [the longest x1 4.92 us: window_back(): jnp.einsum('qhd,khd->hqk', out_grad, value_rows, preferred_element_type=F32)]
    slice x6 -> x0, local copies, waits for them, and re-layouts: 17.3 us -> none  [the longest x3 11 us: shards(): widened_grads = jnp.concatenate((from_above, window_grads[:half]), 0)]
    gather x3 -> x0, local copies, waits for them, and re-layouts: 15.8 us -> none  [the longest x1 5.39 us: shards(): send_grad = jnp.where(filled[:, None], sent_grad[pair_of], zero_value)]
    reduce_sum x5 -> x0, other arithmetic: 12.9 us -> none  [the longest x1 7.98 us: shards(): jnp.sum(returned.reshape(E, group, C, width).astype(jnp.float32), 1)]
    ppermute x4, waiting for transfers between devices: 57.8 us -> 46.9 us  [from_behind(): return lax.ppermute(block, axis, route)]
  transfers between devices with their start and end apart: 5 -> 4, of which waited for: 4 -> 4; matrix products, arithmetic and copies ran while one was open for 2% -> 0% of each run, Pallas kernels for 0% -> 0%
where the time goes in v1:
time: 279 us; the launch traced here: 274 us
  Pallas kernels  168 us (60%)
  waiting for transfers between devices  46.9 us (17%)
  local copies, waits for them, and re-layouts  30.4 us (11%)
  matrix products  17.8 us (6%)
  other arithmetic  6.9 us (2%)
  starting transfers between devices  3.76 us (1%)
    pallas_call x1, Pallas kernels, moe(): pl.pallas_call(moe_kernel, out_shape=jax.ShapeDtypeStruct((256, 1024), BF...  168 us
    ppermute x4, waiting for transfers between devices, from_behind(): return lax.ppermute(block, axis, route)  46.9 us
    unnamed x26, local copies, waits for them, and re-layouts  12.5 us
    another operation x1, local copies, waits for them, and re-layouts, window_back(): parts = window_data.reshape(tokens_in, 4, HEADS, head_size)  7.95 us
    slice x1, local copies, waits for them, and re-layouts, window_back(): value_rows = parts[:, 2]  5.78 us
    sub x1, matrix products, window_back(): expo = jnp.exp(jnp.where(allowed, scores - highest, -1e+30))  5.72 us
  transfers between devices with their start and end apart: 4, of which 4 were waited for; matrix products, arithmetic and copies ran while one was open for 0% of the time, Pallas kernels for 0%

profile of v1, /device:TPU:1, one launch (start us, length us, event | category | flops | bytes accessed | tf_op | source)
XLA Modules:
  0.0 274.1 jit_solution(3994220337548367998)
XLA Ops:
  0.0 1.0 reshape.187
  1.0 0.9 copy.20
  1.9 0.8 reshape.189
  2.7 0.9 copy.21
  3.6 168.0 %moe.1 = bf16[256,1024]{1,0:T(8,128)(2,1)} custom-call(bf16[256,1024]{1,0:T(8,128)(2,1)} %bitcast.122, bf16[256,1024]{1,0:T(8,128)(2,1)} %bitcast.123, f32[256,2]{1,0:T(8,128)} %bitcast.124, s32[256,2]{1,0:T(8,128)} %bitcast.125, bf16[1024,1024]{1,0:T(8,128)(2,1)} %bitcast.118, bf16[1024,1024]{1,0:T(8,128)(2,1)} %bitcast.119, f32[1,1024]{1,0:T(1,128)} %bitcast.128), custom_call_target="tpu_custom_call" | custom-call | tf_op jit(solution)/shard_map/moe/pallas_call | solution.py:365
  171.7 1.8 convolution_convert_fusion.1
  173.5 0.2 fusion.21
  173.7 2.4 collective-permute-start
  176.1 22.1 %collective-permute-done = bf16[16,8,4,1024]{3,1,2,0:T(8,128)(2,1)S(1)} collective-permute-done((bf16[16,8,4,1024]{3,1,2,0:T(8,128)(2,1)S(1)}, bf16[16,8,4,1024]{3,1,2,0:T(8,128)(2,1)S(1)}, u32[]{:S(2)}, u32[]{:S(2)}) %collective-permute-start) | collective-permute-done | bytes 1048608 | tf_op jit(solution)/shard_map/ppermute | solution.py:22
  198.2 0.2 fusion.20
  198.4 1.3 collective-permute-start.1
  199.8 0.1 broadcast_add_fusion
  199.8 0.1 add.45
  199.9 0.1 broadcast_compare_fusion
  200.0 12.8 %collective-permute-done.1 = bf16[8,16,4,1024]{3,1,2,0:T(8,128)(2,1)S(1)} collective-permute-done((bf16[8,16,4,1024]{3,1,2,0:T(8,128)(2,1)S(1)}, bf16[8,16,4,1024]{3,1,2,0:T(8,128)(2,1)S(1)}, u32[]{:S(2)}, u32[]{:S(2)}) %collective-permute-start.1) | collective-permute-done | bytes 1048608 | tf_op jit(solution)/shard_map/ppermute | solution.py:22
  212.8 0.2 pad_maximum_fusion
  213.0 0.2 copy.23
  213.2 7.9 %reshape_reshape.6 = bf16[256,4,32,32]{3,2,0,1:T(8,128)(2,1)} reshape(bf16[16,16,4,1024]{3,1,0,2:T(8,128)(2,1)S(1)} %copy.23) | data formatting | bytes 4194304 | tf_op jit(solution)/shard_map/reshape;reshape | solution.py:398
  221.1 5.8 %fusion.55 = (bf16[256,1,32,32]{3,2,0,1:T(8,128)(2,1)S(1)}, bf16[256,1,32,32]{3,2,0,1:T(8,128)(2,1)}, bf16[256,1,32,32]{3,2,0,1:T(8,128)(2,1)}, bf16[256,1,32,32]{3,2,0,1:T(8,128)(2,1)}) fusion(bf16[256,4,32,32]{3,2,0,1:T(8,128)(2,1)} %reshape_reshape.6), kind=kLoop, calls=%fused_computation.76 | loop fusion | bytes 4194304 | tf_op jit(solution)/shard_map/slice | solution.py:401
  226.9 2.8 %copy.34 = bf16[256,1,32,32]{0,3,2,1:T(8,128)(2,1)S(1)} copy(bf16[256,1,32,32]{3,2,0,1:T(8,128)(2,1)} %get-tuple-element.10) | data formatting | bytes 1048576
  229.7 2.8 %copy.35 = bf16[256,1,32,32]{0,3,2,1:T(8,128)(2,1)S(1)} copy(bf16[256,1,32,32]{3,2,0,1:T(8,128)(2,1)} %get-tuple-element.9) | data formatting | bytes 1048576
  232.5 3.4 %copy.36 = bf16[256,1,32,32]{0,3,2,1:T(8,128)(2,1)} copy(bf16[256,1,32,32]{3,2,0,1:T(8,128)(2,1)} %get-tuple-element.8) | data formatting | bytes 1048576
  235.9 2.4 copy.37
  238.3 5.7 %fusion.57 = (f32[32,256]{1,0:T(8,128)S(1)}, f32[32,256,256]{1,2,0:T(8,128)}) fusion(pred[256,256]{0,1:T(8,128)(4,1)S(1)} %broadcast_compare_fusion, bf16[256,1,32,32]{0,3,2,1:T(8,128)(2,1)S(1)} %copy.35, bf16[256,1,32,32]{0,3,2,1:T(8,128)(2,1)S(1)} %copy.34), kind=kOutput, calls=%fused_computation.78 | convolution fusion | flops 281018624 | bytes 9535488 | tf_op jit(solution)/shard_map/sub | solution.py:406
  244.0 4.9 %multiply_reduce_fusion = (f32[32,256]{1,0:T(8,128)S(1)}, f32[32,256,256]{1,2,0:T(8,128)S(1)}) fusion(f32[32,256,256]{1,2,0:T(8,128)} %get-tuple-element.18, f32[32,256]{1,0:T(8,128)S(1)} %get-tuple-element.17, bf16[256,1,32,32]{0,3,2,1:T(8,128)(2,1)S(1)} %copy-done.5, bf16[256,1,32,32]{0,3,2,1:T(8,128)(2,1)S(1)} %copy-done.4), kind=kOutput, calls=%fused_computation.2 | convolution fusion | flops 140500992 | bytes 17891328 | tf_op jit(solution)/shard_map/qhd,khd->hqk/dot_general | solution.py:412
  248.9 0.9 slice-done.1
  249.8 2.0 multiply_convert_fusion
  251.9 0.8 fusion.16
  252.7 0.0 slice-start.2
  252.7 1.3 fusion.15
  254.0 0.0 slice-start.3
  254.0 1.4 fusion.17
  255.4 0.2 pad_maximum_fusion.1
  255.6 0.2 slice-done.3
  255.8 1.9 convolution_convert_fusion
  257.8 0.0 collective-permute-start.2
  257.8 0.1 convert_reduce_fusion
  257.9 3.1 %collective-permute-done.2 = bf16[8,16,1024]{2,1,0:T(8,128)(2,1)S(1)} collective-permute-done((bf16[8,16,1024]{2,1,0:T(8,128)(2,1)S(1)}, bf16[8,16,1024]{2,1,0:T(8,128)(2,1)S(1)}, u32[]{:S(2)}, u32[]{:S(2)}) %collective-permute-start.2) | collective-permute-done | bytes 262176 | tf_op jit(solution)/shard_map/ppermute | solution.py:22
  261.1 0.7 fusion.52
  261.8 0.0 collective-permute-start.3
  261.8 0.3 multiply_reduce_fusion.1
  262.1 0.1 div.32
  262.2 0.1 rsqrt.13
  262.3 8.9 %collective-permute-done.3 = bf16[16,8,1024]{2,1,0:T(8,128)(2,1)S(1)} collective-permute-done((bf16[16,8,1024]{2,1,0:T(8,128)(2,1)}, bf16[16,8,1024]{2,1,0:T(8,128)(2,1)S(1)}, u32[]{:S(2)}, u32[]{:S(2)}) %collective-permute-start.3) | collective-permute-done | bytes 262176 | tf_op jit(solution)/shard_map/ppermute | solution.py:22
  271.2 0.4 multiply_reduce_fusion.2
  271.6 0.1 div.31
  271.7 0.1 div.34
  271.7 2.3 fusion.30
  (26 shorter events, 0.1 us)
Async XLA Ops:
  0.0 171.7 %copy-start = (bf16[1024,1024]{1,0:T(8,128)(2,1)S(1)}, bf16[1024,1024]{1,0:T(8,128)(2,1)}, u32[]{:S(2)}) copy-start(bf16[1024,1024]{1,0:T(8,128)(2,1)} %param.21) | copy-start | bytes 6291460
  3.6 169.9 %copy-start.3 = (bf16[1,1,16,16,3,1024]{5,3,4,2,1,0:T(8,128)(2,1)S(1)}, bf16[1,1,16,16,3,1024]{5,3,4,2,1,0:T(8,128)(2,1)}, u32[]{:S(2)}) copy-start(bf16[1,1,16,16,3,1024]{5,3,4,2,1,0:T(8,128)(2,1)} %param.15) | copy-start | bytes 4718596
  173.7 24.5 %collective-permute-start = (bf16[16,8,4,1024]{3,1,2,0:T(8,128)(2,1)S(1)}, bf16[16,8,4,1024]{3,1,2,0:T(8,128)(2,1)S(1)}, u32[]{:S(2)}, u32[]{:S(2)}) collective-permute-start(bf16[16,8,4,1024]{3,1,2,0:T(8,128)(2,1)S(1)} %get-tuple-element.14), channel_id=1, source_target_pairs={{1,0},{2,1},{3,2},{4,3},{5,4},{6,5},{7,6},{8,7},{9,8},{10,9},{11,1... | collective-permute-start | bytes 3145736 | tf_op jit(solution)/shard_map/ppermute | solution.py:22
  198.4 14.4 %collective-permute-start.1 = (bf16[8,16,4,1024]{3,1,2,0:T(8,128)(2,1)S(1)}, bf16[8,16,4,1024]{3,1,2,0:T(8,128)(2,1)S(1)}, u32[]{:S(2)}, u32[]{:S(2)}) collective-permute-start(bf16[8,16,4,1024]{3,1,2,0:T(8,128)(2,1)S(1)} %get-tuple-element.12), channel_id=1, source_target_pairs={{16,0},{32,16},{48,32},{64,48},{80,64},{96,80},{112,96},{0,112},{1... | collective-permute-start | bytes 3145736 | tf_op jit(solution)/shard_map/ppermute | solution.py:22
  238.3 5.7 %copy-start.4 = (bf16[256,1,32,32]{0,3,2,1:T(8,128)(2,1)S(1)}, bf16[256,1,32,32]{0,3,2,1:T(8,128)(2,1)}, u32[]{:S(2)}) copy-start(bf16[256,1,32,32]{0,3,2,1:T(8,128)(2,1)} %copy.36) | copy-start | bytes 1572868
  238.3 5.7 %copy-start.5 = (bf16[256,1,32,32]{0,3,2,1:T(8,128)(2,1)S(1)}, bf16[256,1,32,32]{0,3,2,1:T(8,128)(2,1)}, u32[]{:S(2)}) copy-start(bf16[256,1,32,32]{0,3,2,1:T(8,128)(2,1)} %copy.37) | copy-start | bytes 1572868
  244.0 4.9 %slice-start = ((s8[8388608]{0:T(1024)(128)(4,1)}), s8[4194304]{0:T(1024)(128)(4,1)S(1)}, s32[]{:S(2)}) async-start(s8[8388608]{0:T(1024)(128)(4,1)} %bitcast.113), calls=%async_computation | async-start | bytes 8388608
  244.0 5.8 %slice-start.1 = ((s8[8388608]{0:T(1024)(128)(4,1)}), s8[4194304]{0:T(1024)(128)(4,1)S(1)}, s32[]{:S(2)}) async-start(s8[8388608]{0:T(1024)(128)(4,1)} %bitcast.113), calls=%async_computation.1 | async-start | bytes 8388608
  252.7 2.9 %slice-start.2 = ((s8[6291456]{0:T(1024)(128)(4,1)}), s8[4194304]{0:T(1024)(128)(4,1)S(1)}, s32[]{:S(2)}) async-start(s8[6291456]{0:T(1024)(128)(4,1)} %bitcast.129), calls=%async_computation.2 | async-start | bytes 8388608
  254.0 1.8 slice-start.3
  255.8 2.0 copy-start.2
  255.8 15.3 %copy-start.6 = (f32[1024]{0:T(1024)S(1)}, f32[1024]{0:T(1024)}, u32[]{:S(2)}) copy-start(f32[1024]{0:T(1024)} %param.22) | copy-start | bytes 12292
  255.8 18.2 %copy-start.1 = (bf16[1024,1024]{1,0:T(8,128)(2,1)S(1)}, bf16[1024,1024]{1,0:T(8,128)(2,1)}, u32[]{:S(2)}) copy-start(bf16[1024,1024]{1,0:T(8,128)(2,1)} %param.21) | copy-start | bytes 6291460
  257.8 3.3 %collective-permute-start.2 = (bf16[8,16,1024]{2,1,0:T(8,128)(2,1)S(1)}, bf16[8,16,1024]{2,1,0:T(8,128)(2,1)S(1)}, u32[]{:S(2)}, u32[]{:S(2)}) collective-permute-start(bf16[8,16,1024]{2,1,0:T(8,128)(2,1)S(1)} %bitcast.127), channel_id=1, source_target_pairs={{112,0},{0,16},{16,32},{32,48},{48,64},{64,80},{80,96},{96,112},{1... | collective-permute-start | bytes 786440 | tf_op jit(solution)/shard_map/ppermute | solution.py:22
  261.8 9.3 %collective-permute-start.3 = (bf16[16,8,1024]{2,1,0:T(8,128)(2,1)}, bf16[16,8,1024]{2,1,0:T(8,128)(2,1)S(1)}, u32[]{:S(2)}, u32[]{:S(2)}) collective-permute-start(bf16[16,8,1024]{2,1,0:T(8,128)(2,1)} %fusion.52), channel_id=1, source_target_pairs={{15,0},{0,1},{1,2},{2,3},{3,4},{4,5},{5,6},{6,7},{7,8},{8,9},{9,10... | collective-permute-start | bytes 786440 | tf_op jit(solution)/shard_map/ppermute | solution.py:22

commit v2 on v1

--- a/solution.py
+++ b/solution.py
@@ -16,12 +16,6 @@
 PIECES = 8
 
 
-def from_behind(block, axis, distance):
-    devices = range(lax.axis_size(axis))
-    route = [((i - distance) % len(devices), i) for i in devices]
-    return lax.ppermute(block, axis, route)
-
-
 def layer_stats(values):
     floats = values.astype(F32)
     centred = floats - jnp.mean(floats, -1, keepdims=True)
@@ -76,13 +70,18 @@
     return (2 * y + c, 4 * x + z)
 
 
-def moe_kernel(
+def block_kernel(
     mid_ref,
     grad_ref,
+    block_ref,
+    qkv_ref,
     gates_ref,
     ids_ref,
     w_in_ref,
     w_out_ref,
+    w_qkv_ref,
+    w_proj_ref,
+    norm1_ref,
     norm2_ref,
     out_ref,
     w_first,
@@ -90,9 +89,19 @@
     outgoing,
     arrived,
     total,
-    ret_out,
     ret_in,
     choice,
+    probs,
+    window_out,
+    window_in,
+    context_out,
+    context_in,
+    heads_grad,
+    final_out,
+    final_in,
+    l_sem,
+    h_send,
+    h_recv,
     w_send,
     w_recv,
     d_send,
@@ -114,6 +123,12 @@
         differs = lax.rem(eb + pair, 2)
         return place(ex, ey, c, z + differs * (3 - 2 * z))
 
+    row, col = lax.axis_index("row"), lax.axis_index("col")
+    up, left = lax.rem(row + 7, 8), lax.rem(col + 15, 16)
+    down, right = lax.rem(row + 1, 8), lax.rem(col + 1, 16)
+    back = ((up, left), (up, col), (row, left))
+    ahead = (None, (row, right), (down, col), (down, right))
+
     barrier = pltpu.get_barrier_semaphore()
 
     def greet(e, carry):
@@ -124,9 +139,10 @@
         return carry
 
     lax.fori_loop(0, E, greet, 0)
-    for where in (twin, place(x, y, 0, u), place(x, y, 1, u), place(x, y, other, w)):
+    near = (twin, place(x, y, 0, u), place(x, y, 1, u), place(x, y, other, w))
+    for where in near + back + ahead[1:]:
         pl.semaphore_signal(barrier, inc=1, device_id=where, device_id_type=MESH)
-    pl.semaphore_wait(barrier, E - 1 + 4)
+    pl.semaphore_wait(barrier, E - 1 + 10)
 
     def source(which, h):
         if which == 0:
@@ -235,6 +251,57 @@
     lax.fori_loop(0, 4, dispatch, 0)
     total[...] = jnp.zeros_like(total)
 
+    def ship_quadrant(stage, src, dst, q, where):
+        return pltpu.make_async_remote_copy(
+            src_ref=src.at[q],
+            dst_ref=dst.at[3 - q],
+            send_sem=h_send.at[stage, q],
+            recv_sem=h_recv.at[stage, 3 - q],
+            device_id=where,
+            device_id_type=MESH,
+        )
+
+    def quadrant_landed(stage, dst, q):
+        pltpu.make_async_copy(dst.at[q], dst.at[q], h_recv.at[stage, q]).wait()
+
+    for part in range(3):
+        rows = to_quadrants(qkv_ref[:, part].reshape(256, 1024).astype(F32)).astype(BF16)
+        window_out[:, part] = rows.reshape(4, 64, 1024)
+        window_in[0, part] = rows[192:]
+    for q in range(3):
+        ship_quadrant(0, window_out, window_in, q, back[q]).start()
+    for q in range(1, 4):
+        quadrant_landed(0, window_in, q)
+
+    last_row = (row == 7).astype(jnp.int32)
+    last_col = (col == 15).astype(jnp.int32)
+
+    def labels(shape, dim):
+        quadrant = lax.div(lax.broadcasted_iota(jnp.int32, shape, dim), 64)
+        return lax.div(quadrant, 2) * (2 * last_row) + lax.rem(quadrant, 2) * last_col
+
+    allowed = labels((256, 256), 0) == labels((256, 256), 1)
+    shut = jnp.where(allowed, 0.0, -1e30)
+    scale = 32**-0.5
+    head_of = lax.div(lax.broadcasted_iota(jnp.int32, (256, 128), 1), 32)
+
+    def of_head(h, rows):
+        return jnp.where(head_of == h, rows, jnp.zeros_like(rows))
+
+    def window_part(part, lanes_at):
+        return window_in[:, part, :, lanes_at].reshape(256, 128)
+
+    def softmax_group(group, carry):
+        lanes_at = pl.ds(pl.multiple_of(group * 128, 128), 128)
+        query, key = window_part(0, lanes_at), window_part(1, lanes_at)
+        for h in range(4):
+            scores = dot(of_head(h, key), query, (1, 1)) * scale + shut
+            expo = jnp.exp(scores - jnp.max(scores, 0, keepdims=True))
+            probs[4 * group + h] = (expo * (1.0 / jnp.sum(expo, 0, keepdims=True))).astype(BF16)
+        return carry
+
+    lax.fori_loop(0, HEADS // 4, softmax_group, 0)
+
     def landed(which, piece):
         pltpu.make_async_copy(
             store[which].at[piece], store[which].at[piece], w_recv.at[which, piece]
@@ -290,9 +357,18 @@
     for which in range(2):
         landed(which, 2 * v + other)
 
+    def rows_gone(e, carry):
+        @pl.when(e != me)
+        def _():
+            ship_rows(e).wait_send()
+
+        return carry
+
+    lax.fori_loop(0, E, rows_gone, 0)
+
     def ship_back(m):
         return pltpu.make_async_remote_copy(
-            src_ref=ret_out.at[m],
+            src_ref=outgoing.at[m, 0],
             dst_ref=ret_in.at[me],
             send_sem=r_send.at[m],
             recv_sem=r_recv.at[me],
@@ -304,7 +380,7 @@
         block = lax.rem(y + step, 4)
         at = pl.ds(pl.multiple_of(block * 256, 256), 256)
         done = total[at] + product(2 * v + other, 256, block * 8)
-        ret_out[pl.ds(block * 8, 8)] = done.astype(BF16).reshape(8, C, 1024)
+        outgoing[pl.ds(block * 8, 8), 0] = done.astype(BF16).reshape(8, C, 1024)
 
         def send_one(k, carry):
             m = block * 8 + lax.rem(4 * pair + x + k, 8)
@@ -316,7 +392,7 @@
             @pl.when(m == me)
             def _():
                 pltpu.make_async_copy(
-                    ret_out.at[me], ret_in.at[me], r_recv.at[me]
+                    outgoing.at[me, 0], ret_in.at[me], r_recv.at[me]
                 ).start()
 
             return carry
@@ -325,47 +401,120 @@
 
     lax.fori_loop(0, 4, last, 0)
 
-    def back_landed(m, carry):
-        pltpu.make_async_copy(ret_in.at[m], ret_in.at[m], r_recv.at[m]).wait()
-        return carry
-
-    lax.fori_loop(0, E, back_landed, 0)
-    normed_grad = dot(choice[...], ret_in[...].reshape(E * C, 1024))
-    mid_grad = grad + norm_back(normed_grad, mid_hat, mid_inverse, norm2)
-    out_ref[...] = from_quadrants(mid_grad).astype(BF16)
-
-    def sent_all(e, carry):
-        @pl.when(e != me)
-        def _():
-            ship_rows(e).wait_send()
-            ship_back(e).wait_send()
-
-        return carry
-
-    lax.fori_loop(0, E, sent_all, 0)
-
-    def left(which, send_at):
+    def gone(which, send_at):
         ship(which, store[which].at[0], 0, send_at, twin).wait_send()
 
     for which in range(2):
         for send_at in (0, 1, 4, 5, 6, 7):
-            left(which, send_at)
+            gone(which, send_at)
 
     @pl.when(inside)
     def _():
         for which in range(2):
             for send_at in (2, 3):
-                left(which, send_at)
-
-
-def moe(mid, grad, gates, ids, w_in, w_out, norm2):
+                gone(which, send_at)
+
+    loads = [
+        pltpu.make_async_copy(
+            w_proj_ref.at[pl.ds(k * HID, HID), :], w_second.at[k], l_sem.at[k]
+        )
+        for k in range(2)
+    ] + [
+        pltpu.make_async_copy(
+            w_qkv_ref.at[:, pl.ds(k * HID, HID)], w_first.at[k], l_sem.at[2 + k]
+        )
+        for k in range(6)
+    ]
+    for load in loads:
+        load.start()
+
+    def back_landed(m, carry):
+        pltpu.make_async_copy(ret_in.at[m], ret_in.at[m], r_recv.at[m]).wait()
+        return carry
+
+    lax.fori_loop(0, E, back_landed, 0)
+    normed_grad = dot(choice[...], ret_in[...].reshape(E * C, 1024))
+    mid_grad = grad + norm_back(normed_grad, mid_hat, mid_inverse, norm2)
+    mid_grad = mid_grad.astype(BF16)
+
+    for load in loads:
+        load.wait()
+    context_grad = jnp.concatenate(
+        [dot(mid_grad, w_second[k], (1, 1)).astype(BF16) for k in range(2)], 1
+    )
+    context_out[...] = context_grad.reshape(4, 64, 1024)
+    for q in range(3):
+        ship_quadrant(1, context_out, context_in, q, back[q]).start()
+    context_in[0] = context_grad[192:]
+    in_hat, in_inverse = layer_stats(to_quadrants(block_ref[...].astype(F32)))
+    for q in range(1, 4):
+        quadrant_landed(1, context_in, q)
+
+    def heads_back(group, carry):
+        begin = pl.multiple_of(group * 128, 128)
+        lanes_at = pl.ds(begin, 128)
+        query, key, value = (window_part(part, lanes_at) for part in range(3))
+        out_grad = context_in[:, :, lanes_at].reshape(256, 128)
+        sums = [jnp.zeros((256, 128), F32)] * 3
+        for h in range(4):
+            prob = probs[4 * group + h]
+            prob_f = prob.astype(F32)
+            prob_grad = dot(of_head(h, value), out_grad, (1, 1))
+            row_total = jnp.sum(prob_f * prob_grad, 0, keepdims=True)
+            score_grad = (prob_f * (prob_grad - row_total)).astype(BF16)
+            sums = [
+                sums[0] + dot(score_grad, of_head(h, key), (0, 0)),
+                sums[1] + dot(score_grad, of_head(h, query)),
+                sums[2] + dot(prob, of_head(h, out_grad)),
+            ]
+        for part, factor in enumerate((scale, scale, 1.0)):
+            at = pl.ds(pl.multiple_of(part * 1024 + begin, 128), 128)
+            heads_grad[:, at] = (sums[part] * factor).astype(BF16)
+        return carry
+
+    lax.fori_loop(0, HEADS // 4, heads_back, 0)
+
+    def project(step, carry):
+        at = pl.ds(pl.multiple_of(step * 256, 256), 256)
+        part = sum(
+            dot(heads_grad[:, k * HID : (k + 1) * HID], w_first[k, at, :], (1, 1))
+            for k in range(6)
+        )
+        final_out[:, :, at] = part.astype(BF16).reshape(4, 64, 256)
+        return carry
+
+    lax.fori_loop(0, 4, project, 0)
+    for q in range(1, 4):
+        ship_quadrant(2, final_out, final_in, q, ahead[q]).start()
+    final_in[3] = final_out[0]
+    for q in range(3):
+        quadrant_landed(2, final_in, q)
+    upstream = final_in[...].reshape(256, 1024).astype(F32)
+    result = mid_grad.astype(F32) + norm_back(upstream, in_hat, in_inverse, norm1_ref[...])
+    out_ref[...] = from_quadrants(result).astype(BF16)
+
+    def sent_all(e, carry):
+        @pl.when(e != me)
+        def _():
+            ship_back(e).wait_send()
+
+        return carry
+
+    lax.fori_loop(0, E, sent_all, 0)
+    for q in range(3):
+        ship_quadrant(0, window_out, window_in, q, back[q]).wait_send()
+        ship_quadrant(1, context_out, context_in, q, back[q]).wait_send()
+        ship_quadrant(2, final_out, final_in, q + 1, ahead[q + 1]).wait_send()
+
+
+def block(mid, grad, block_in, qkv, gates, ids, w_in, w_out, w_qkv, w_proj, norm1, norm2):
     vmem = pl.BlockSpec(memory_space=pltpu.VMEM)
     anywhere = pl.BlockSpec(memory_space=pl.ANY)
     dma = pltpu.SemaphoreType.DMA
     return pl.pallas_call(
-        moe_kernel,
+        block_kernel,
         out_shape=jax.ShapeDtypeStruct((256, 1024), BF16),
-        in_specs=[vmem, vmem, vmem, vmem, anywhere, anywhere, vmem],
+        in_specs=[vmem] * 6 + [anywhere] * 4 + [vmem] * 2,
         out_specs=vmem,
         scratch_shapes=[
             pltpu.VMEM((PIECES, 1024, HID), BF16),
@@ -374,8 +523,18 @@
             pltpu.VMEM((E, 2, C, 1024), BF16),
             pltpu.VMEM((E * C, 1024), F32),
             pltpu.VMEM((E, C, 1024), BF16),
-            pltpu.VMEM((E, C, 1024), BF16),
             pltpu.VMEM((256, E * C), BF16),
+            pltpu.VMEM((HEADS, 256, 256), BF16),
+            pltpu.VMEM((4, 3, 64, 1024), BF16),
+            pltpu.VMEM((4, 3, 64, 1024), BF16),
+            pltpu.VMEM((4, 64, 1024), BF16),
+            pltpu.VMEM((4, 64, 1024), BF16),
+            pltpu.VMEM((256, 3072), BF16),
+            pltpu.VMEM((4, 64, 1024), BF16),
+            pltpu.VMEM((4, 64, 1024), BF16),
+            dma((8,)),
+            dma((3, 4)),
+            dma((3, 4)),
             dma((2, 8)),
             dma((2, 8)),
             dma((E,)),
@@ -384,41 +543,10 @@
             dma((E,)),
         ],
         compiler_params=pltpu.CompilerParams(
-            collective_id=0, has_side_effects=True, vmem_limit_bytes=60 * 1024 * 1024
+            collective_id=0, has_side_effects=True, vmem_limit_bytes=62 * 1024 * 1024
         ),
-        name="moe",
-    )(mid, grad, gates, ids, w_in, w_out, norm2)
-
-
-def window_back(window_data, labels):
-    tokens_in = window_data.shape[0]
-    width = window_data.shape[2]
-    head_size = width // HEADS
-    scale = head_size ** (-0.5)
-    parts = window_data.reshape(tokens_in, 4, HEADS, head_size)
-    query = parts[:, 0]
-    key_rows = parts[:, 1]
-    value_rows = parts[:, 2]
-    out_grad = parts[:, 3]
-    scores = jnp.einsum("qhd,khd->hqk", query, key_rows, preferred_element_type=F32) * scale
-    allowed = (labels[:, None] == labels[None, :])[None, :, :]
-    highest = jnp.max(jnp.where(allowed, scores, -1e30), -1, keepdims=True)
-    expo = jnp.exp(jnp.where(allowed, scores - highest, -1e30))
-    probs = expo / jnp.sum(expo, -1, keepdims=True)
-    probs_b = probs.astype(BF16)
-    value_grad = jnp.einsum(
-        "hqk,qhd->khd", probs_b, out_grad, preferred_element_type=F32
-    ).astype(BF16)
-    prob_grad = jnp.einsum("qhd,khd->hqk", out_grad, value_rows, preferred_element_type=F32)
-    row_total = jnp.sum(probs * prob_grad, -1, keepdims=True)
-    score_grad = (probs * (prob_grad - row_total)).astype(BF16)
-    query_grad = (
-        jnp.einsum("hqk,khd->qhd", score_grad, key_rows, preferred_element_type=F32) * scale
-    ).astype(BF16)
-    key_grad = (
-        jnp.einsum("hqk,qhd->khd", score_grad, query, preferred_element_type=F32) * scale
-    ).astype(BF16)
-    return jnp.stack((query_grad, key_grad, value_grad), 1).reshape(tokens_in, 3, width)
+        name="block",
+    )(mid, grad, block_in, qkv, gates, ids, w_in, w_out, w_qkv, w_proj, norm1, norm2)
 
 
 def shards(
@@ -432,44 +560,21 @@
     def columns(a):
         return a.reshape(2, half, 2, half, 2).transpose(0, 2, 1, 3, 4).reshape(count, 2)
 
-    mid_grad = moe(
+    result = block(
         mid.reshape(count, width),
         grad_out.reshape(count, width),
+        block_in.reshape(count, width),
+        qkv.reshape(window, window, 3, width).transpose(0, 2, 1, 3),
         columns(gates),
         columns(expert_ids),
         w_in[0],
         w_out[0],
+        w_qkv,
+        w_proj,
+        norm1.reshape(1, width),
         norm2.reshape(1, width),
     )
-    context_grad = jnp.einsum("td,ed->te", mid_grad, w_proj, preferred_element_type=F32).astype(
-        BF16
-    )
-    stacked = jnp.concatenate(
-        (qkv.reshape(window, window, 3, width), context_grad.reshape(window, window, 1, width)), 2
-    )
-    right_part = from_behind(stacked[:, :half], "col", -1)
-    widened = jnp.concatenate((stacked[:, half:], right_part), 1)
-    lower_part = from_behind(widened[:half], "row", -1)
-    shifted = jnp.concatenate((widened[half:], lower_part), 0)
-    row_last = lax.axis_index("row") == lax.axis_size("row") - 1
-    col_last = lax.axis_index("col") == lax.axis_size("col") - 1
-    lower_half = jnp.arange(window) >= half
-    row_label = (row_last & lower_half).astype(jnp.int32)
-    col_label = (col_last & lower_half).astype(jnp.int32)
-    labels = (row_label[:, None] * 2 + col_label[None, :]).reshape(count)
-    window_grads = window_back(shifted.reshape(count, 4, width), labels)
-    window_grads = jnp.einsum(
-        "tc,dc->td", window_grads.reshape(count, 3 * width), w_qkv, preferred_element_type=F32
-    )
-    window_grads = window_grads.astype(BF16).reshape(window, window, width)
-    from_above = from_behind(window_grads[half:], "row", 1)
-    widened_grads = jnp.concatenate((from_above, window_grads[:half]), 0)
-    from_left = from_behind(widened_grads[:, half:], "col", 1)
-    input_normed_grad = jnp.concatenate((from_left, widened_grads[:, :half]), 1)
-    input_normed_grad = input_normed_grad.reshape(count, width).astype(F32)
-    in_hat, in_inverse = layer_stats(block_in.reshape(count, width))
-    result = mid_grad.astype(F32) + norm_back(input_normed_grad, in_hat, in_inverse, norm1)
-    return result.astype(BF16).reshape(grad_out.shape)
+    return result.reshape(grad_out.shape)
 
 
 def solution(mesh):

time: 279 us -> 226 us (0.81); the launches traced: 274 us -> 225 us
  Pallas kernels: 168 us -> 220 us
  waiting for transfers between devices: 46.9 us -> 0 us
  local copies, waits for them, and re-layouts: 30.4 us -> 5.34 us
  matrix products: 17.8 us -> 0 us
  other arithmetic: 6.9 us -> 0 us
  starting transfers between devices: 3.76 us -> 0 us
    pallas_call x1, Pallas kernels: 168 us -> 220 us  [block(): pl.pallas_call(block_kernel, out_shape=jax.ShapeDtypeStruct((256, 1024),...]
    ppermute x4 -> x0, waiting for transfers between devices: 46.9 us -> none  [from_behind(): return lax.ppermute(block, axis, route)]
    dot_general x6 -> x0, matrix products: 12.1 us -> none  [the longest x1 4.92 us: window_back(): jnp.einsum('qhd,khd->hqk', out_grad, value_rows, preferred_element_type=F32)]
    unnamed x26 -> x1, local copies, waits for them, and re-layouts: 12.5 us -> 1.88 us
    another operation x1 -> x0, local copies, waits for them, and re-layouts: 7.95 us -> none  [window_back(): parts = window_data.reshape(tokens_in, 4, HEADS, head_size)]
    slice x2 -> x0, local copies, waits for them, and re-layouts: 5.81 us -> none  [the longest x1 5.78 us: window_back(): value_rows = parts[:, 2]]
    sub x1 -> x0, matrix products: 5.72 us -> none  [window_back(): expo = jnp.exp(jnp.where(allowed, scores - highest, -1e+30))]
    convert_element_type x3 -> x0, other arithmetic: 4.32 us -> none  [the longest x1 2.31 us: shards(): return result.astype(BF16).reshape(grad_out.shape)]
  transfers between devices with their start and end apart: 4 -> 0, of which waited for: 4 -> 0; matrix products, arithmetic and copies ran while one was open for 0% -> 0% of each run, Pallas kernels for 0% -> 0%
where the time goes in v2:
time: 226 us; the launch traced here: 225 us
  Pallas kernels  220 us (97%)
  local copies, waits for them, and re-layouts  5.34 us (2%)
    pallas_call x1, Pallas kernels, block(): pl.pallas_call(block_kernel, out_shape=jax.ShapeDtypeStruct((256, 1024),...  220 us

profile of v2, /device:TPU:1, one launch (start us, length us, event | category | flops | bytes accessed | tf_op | source)
XLA Modules:
  0.0 225.3 jit_solution(14171049822529347743)
XLA Ops:
  0.0 0.8 reshape.37
  0.8 0.8 reshape.39
  1.6 0.9 copy.14
  2.5 0.9 copy.13
  3.5 219.9 %block.1 = bf16[256,1024]{1,0:T(8,128)(2,1)} custom-call(bf16[256,1024]{1,0:T(8,128)(2,1)} %bitcast.27, bf16[256,1024]{1,0:T(8,128)(2,1)} %bitcast.28, bf16[256,1024]{1,0:T(8,128)(2,1)} %bitcast.29, bf16[16,3,16,1024]{3,2,1,0:T(8,128)(2,1)} %bitcast.24, f32[256,2]{1,0:T(8,128)} %bitcast.26, s32[256,2]{1,0:T(8,128)} %bitcast.25, bf16[1024,1024]{1,0:T(8,128)(2,1)} %bitcast.21, ...), custom_call_target="tpu_custom_call" | custom-call | tf_op jit(solution)/shard_map/block/pallas_call | solution.py:514
  223.4 1.9 copy.16

commit v3 on v2

--- a/solution.py
+++ b/solution.py
@@ -75,8 +75,7 @@
     grad_ref,
     block_ref,
     qkv_ref,
-    gates_ref,
-    ids_ref,
+    routes_ref,
     w_in_ref,
     w_out_ref,
     w_qkv_ref,
@@ -86,6 +85,9 @@
     out_ref,
     w_first,
     w_second,
+    mate_mid,
+    mate_grad,
+    mate_routes,
     outgoing,
     arrived,
     total,
@@ -102,6 +104,8 @@
     l_sem,
     h_send,
     h_recv,
+    m_send,
+    m_recv,
     w_send,
     w_recv,
     d_send,
@@ -117,6 +121,7 @@
     other = 1 - c
     twin = place(x, y, other, z)
     me = 8 * y + 4 * pair + x
+    mate = 8 * y + 4 * (1 - pair) + x
 
     def member(e):
         ex, ey, eb = lax.rem(e, 4), lax.div(e, 8), lax.rem(lax.div(e, 4), 2)
@@ -168,6 +173,26 @@
         )
 
     inside = c == pair
+    outside = jnp.logical_not(inside)
+
+    tile = (
+        (mid_ref, mate_mid),
+        (grad_ref, mate_grad),
+        (routes_ref, mate_routes),
+    )
+
+    def ship_tile(n):
+        return pltpu.make_async_remote_copy(
+            src_ref=tile[n][0],
+            dst_ref=tile[n][1],
+            send_sem=m_send.at[n],
+            recv_sem=m_recv.at[n],
+            device_id=place(x, y, c, w),
+            device_id_type=MESH,
+        )
+
+    for n in range(3):
+        ship_tile(n).start()
 
     @pl.when(inside)
     def _():
@@ -179,76 +204,82 @@
                 ship(which, source(which, h), 2 * z + h, 2 + h, twin).start()
                 local(which, h).start()
 
-    @pl.when(jnp.logical_not(inside))
-    def _():
-        for h in range(2):
-            for which in range(2):
-                ship(which, source(which, h), 2 * z + h, h, place(x, y, h, w)).start()
+    def cross(which, h):
+        return ship(which, source(which, h), 2 * z + h, h, place(x, y, h, w))
 
     norm2 = norm2_ref[...]
-    grad = to_quadrants(grad_ref[...].astype(F32))
-    mid_hat, mid_inverse = layer_stats(to_quadrants(mid_ref[...].astype(F32)))
-    normed = (mid_hat * norm2).astype(BF16)
-    gates = gates_ref[...]
-    ids = ids_ref[...]
-    sent = [(gates[:, k : k + 1] * grad).astype(BF16) for k in range(2)]
-    lanes = lax.broadcasted_iota(jnp.int32, (256, E), 1)
-    hots = [ids[:, k : k + 1] == lanes for k in range(2)]
-    before = (
-        lax.broadcasted_iota(jnp.int32, (256, 256), 0)
-        > lax.broadcasted_iota(jnp.int32, (256, 256), 1)
-    ).astype(BF16)
-    hot_f = [h.astype(F32) for h in hots]
-    ranks = [dot(before, h.astype(BF16)) for h in hot_f]
-    ranks[1] = ranks[1] + jnp.sum(hot_f[0], 0, keepdims=True)
-    slots = [
-        ids[:, k : k + 1] * C
-        + jnp.sum(hot_f[k] * ranks[k], 1, keepdims=True).astype(jnp.int32)
-        for k in range(2)
-    ]
+
+    def prepare(mid_rows, grad_rows, routes):
+        grad = to_quadrants(grad_rows.astype(F32))
+        mid_hat, mid_inverse = layer_stats(to_quadrants(mid_rows.astype(F32)))
+        normed = (mid_hat * norm2).astype(BF16)
+        ids = routes[:, 2:4].astype(jnp.int32)
+        sent = [(routes[:, k : k + 1] * grad).astype(BF16) for k in range(2)]
+        lanes = lax.broadcasted_iota(jnp.int32, (256, E), 1)
+        hots = [(ids[:, k : k + 1] == lanes).astype(F32) for k in range(2)]
+        before = (
+            lax.broadcasted_iota(jnp.int32, (256, 256), 0)
+            > lax.broadcasted_iota(jnp.int32, (256, 256), 1)
+        ).astype(BF16)
+        ranks = [dot(before, h.astype(BF16)) for h in hots]
+        ranks[1] = ranks[1] + jnp.sum(hots[0], 0, keepdims=True)
+        slots = [
+            ids[:, k : k + 1] * C
+            + jnp.sum(hots[k] * ranks[k], 1, keepdims=True).astype(jnp.int32)
+            for k in range(2)
+        ]
+        return grad, mid_hat, mid_inverse, normed, sent, slots
+
+    def ship_rows(at, origin, ex, ey):
+        return pltpu.make_async_remote_copy(
+            src_ref=outgoing.at[at],
+            dst_ref=arrived.at[origin],
+            send_sem=d_send.at[at],
+            recv_sem=d_recv.at[origin],
+            device_id=place(ex, ey, c, z),
+            device_id_type=MESH,
+        )
+
+    narrow = lax.broadcasted_iota(jnp.int32, (256, 128), 1)
+
+    def dispatch(normed, sent, slots, bit, origin):
+        def one(step, carry):
+            ey = lax.rem(y + step, 4)
+            base = (8 * ey + 4 * pair) * C
+            picks = [(slots[k] == narrow + base).astype(BF16) for k in range(2)]
+            rows_n = dot(picks[0] + picks[1], normed, (0, 0))
+            rows_g = dot(picks[0], sent[0], (0, 0)) + dot(picks[1], sent[1], (0, 0))
+            begin = 8 * ey + 4 * bit
+            outgoing[pl.ds(begin, 4), 0] = rows_n.astype(BF16).reshape(4, C, 1024)
+            outgoing[pl.ds(begin, 4), 1] = rows_g.astype(BF16).reshape(4, C, 1024)
+
+            def send_one(k, carry):
+                ex = lax.rem(x + k, 4)
+                at = begin + ex
+                here = at == 8 * y + 4 * bit + x
+
+                @pl.when(jnp.logical_not(here))
+                def _():
+                    ship_rows(at, origin, ex, ey).start()
+
+                @pl.when(here)
+                def _():
+                    pltpu.make_async_copy(
+                        outgoing.at[at], arrived.at[origin], d_recv.at[origin]
+                    ).start()
+
+                return carry
+
+            return lax.fori_loop(0, 4, send_one, carry)
+
+        lax.fori_loop(0, 4, one, 0)
+
+    grad, mid_hat, mid_inverse, normed, sent, slots = prepare(
+        mid_ref[...], grad_ref[...], routes_ref[...]
+    )
     wide = lax.broadcasted_iota(jnp.int32, (256, E * C), 1)
     choice[...] = ((slots[0] == wide) | (slots[1] == wide)).astype(BF16)
-
-    def ship_rows(e):
-        return pltpu.make_async_remote_copy(
-            src_ref=outgoing.at[e],
-            dst_ref=arrived.at[me],
-            send_sem=d_send.at[e],
-            recv_sem=d_recv.at[me],
-            device_id=member(e),
-            device_id_type=MESH,
-        )
-
-    def keep_rows():
-        return pltpu.make_async_copy(outgoing.at[me], arrived.at[me], d_recv.at[me])
-
-    narrow = lax.broadcasted_iota(jnp.int32, (256, 256), 1)
-
-    def dispatch(step, carry):
-        block = lax.rem(y + step, 4)
-        base = block * 256
-        picks = [(slots[k] == narrow + base).astype(BF16) for k in range(2)]
-        rows_n = dot(picks[0] + picks[1], normed, (0, 0))
-        rows_g = dot(picks[0], sent[0], (0, 0)) + dot(picks[1], sent[1], (0, 0))
-        outgoing[pl.ds(block * 8, 8), 0] = rows_n.astype(BF16).reshape(8, C, 1024)
-        outgoing[pl.ds(block * 8, 8), 1] = rows_g.astype(BF16).reshape(8, C, 1024)
-
-        def send_one(k, carry):
-            e = block * 8 + lax.rem(4 * pair + x + k, 8)
-
-            @pl.when(e != me)
-            def _():
-                ship_rows(e).start()
-
-            @pl.when(e == me)
-            def _():
-                keep_rows().start()
-
-            return carry
-
-        return lax.fori_loop(0, 8, send_one, carry)
-
-    lax.fori_loop(0, 4, dispatch, 0)
+    dispatch(normed, sent, slots, pair, me)
     total[...] = jnp.zeros_like(total)
 
     def ship_quadrant(stage, src, dst, q, where):
@@ -270,6 +301,21 @@
         window_in[0, part] = rows[192:]
     for q in range(3):
         ship_quadrant(0, window_out, window_in, q, back[q]).start()
+    for n in range(3):
+        ship_tile(n).wait_send()
+
+    @pl.when(outside)
+    def _():
+        for h in range(2):
+            cross(0, h).start()
+
+    for n in range(3):
+        pltpu.make_async_copy(tile[n][1], tile[n][1], m_recv.at[n]).wait()
+    _, _, _, normed_m, sent_m, slots_m = prepare(
+        mate_mid[...], mate_grad[...], mate_routes[...]
+    )
+    dispatch(normed_m, sent_m, slots_m, 1 - pair, mate)
+
     for q in range(1, 4):
         quadrant_landed(0, window_in, q)
 
@@ -307,11 +353,10 @@
             store[which].at[piece], store[which].at[piece], w_recv.at[which, piece]
         ).wait()
 
-    def pass_on(piece, send_at, targets):
-        for which in range(2):
-            landed(which, piece)
-            for n, where in enumerate(targets):
-                ship(which, store[which].at[piece], piece, send_at + n, where).start()
+    def pass_on(which, piece, send_at, targets):
+        landed(which, piece)
+        for n, where in enumerate(targets):
+            ship(which, store[which].at[piece], piece, send_at + n, where).start()
 
     def product(piece, rows, begin):
         count = rows // C
@@ -332,35 +377,47 @@
 
         lax.fori_loop(0, 1024 // rows, one, 0)
 
-    pass_on(2 * w + c, 4, (place(x, y, c, u), twin))
-    pass_on(2 * u + c, 6, (twin,))
+    @pl.when(outside)
+    def _():
+        for h in range(2):
+            cross(0, h).wait_send()
+            cross(1, h).start()
+
+    onward = (place(x, y, c, u), twin)
+    pass_on(0, 2 * w + c, 4, onward)
+    for which in range(2):
+        pass_on(which, 2 * u + c, 6, (twin,))
 
     def rows_landed(m, carry):
         pltpu.make_async_copy(arrived.at[m], arrived.at[m], d_recv.at[m]).wait()
         return carry
 
     lax.fori_loop(0, E, rows_landed, 0)
-    for h in range(2):
-        for which in range(2):
-            landed(which, 2 * z + h)
-        whole(2 * z + h)
+    for which in range(2):
+        landed(which, 2 * z)
+    whole(2 * z)
+    pass_on(1, 2 * w + c, 4, onward)
+    for which in range(2):
+        landed(which, 2 * z + 1)
+    whole(2 * z + 1)
     whole(2 * u + c)
     whole(2 * w + c)
+    pass_on(0, 2 * v + c, 7, (twin,))
     for which in range(2):
         landed(which, 2 * u + other)
     whole(2 * u + other)
     for which in range(2):
         landed(which, 2 * w + other)
     whole(2 * w + other)
-    pass_on(2 * v + c, 7, (twin,))
+    pass_on(1, 2 * v + c, 7, (twin,))
     whole(2 * v + c)
     for which in range(2):
         landed(which, 2 * v + other)
 
-    def rows_gone(e, carry):
-        @pl.when(e != me)
+    def rows_gone(at, carry):
+        @pl.when((at != me) & (at != mate))
         def _():
-            ship_rows(e).wait_send()
+            ship_rows(at, me, x, y).wait_send()
 
         return carry
 
@@ -405,14 +462,19 @@
         ship(which, store[which].at[0], 0, send_at, twin).wait_send()
 
     for which in range(2):
-        for send_at in (0, 1, 4, 5, 6, 7):
+        for send_at in (4, 5, 6, 7):
             gone(which, send_at)
 
     @pl.when(inside)
     def _():
         for which in range(2):
-            for send_at in (2, 3):
+            for send_at in range(4):
                 gone(which, send_at)
+
+    @pl.when(outside)
+    def _():
+        for send_at in range(2):
+            gone(1, send_at)
 
     loads = [
         pltpu.make_async_copy(
@@ -507,18 +569,21 @@
         ship_quadrant(2, final_out, final_in, q + 1, ahead[q + 1]).wait_send()
 
 
-def block(mid, grad, block_in, qkv, gates, ids, w_in, w_out, w_qkv, w_proj, norm1, norm2):
+def block(mid, grad, block_in, qkv, routes, w_in, w_out, w_qkv, w_proj, norm1, norm2):
     vmem = pl.BlockSpec(memory_space=pltpu.VMEM)
     anywhere = pl.BlockSpec(memory_space=pl.ANY)
     dma = pltpu.SemaphoreType.DMA
     return pl.pallas_call(
         block_kernel,
         out_shape=jax.ShapeDtypeStruct((256, 1024), BF16),
-        in_specs=[vmem] * 6 + [anywhere] * 4 + [vmem] * 2,
+        in_specs=[vmem] * 5 + [anywhere] * 4 + [vmem] * 2,
         out_specs=vmem,
         scratch_shapes=[
             pltpu.VMEM((PIECES, 1024, HID), BF16),
             pltpu.VMEM((PIECES, HID, 1024), BF16),
+            pltpu.VMEM((256, 1024), BF16),
+            pltpu.VMEM((256, 1024), BF16),
+            pltpu.VMEM((256, 128), F32),
             pltpu.VMEM((E, 2, C, 1024), BF16),
             pltpu.VMEM((E, 2, C, 1024), BF16),
             pltpu.VMEM((E * C, 1024), F32),
@@ -535,6 +600,8 @@
             dma((8,)),
             dma((3, 4)),
             dma((3, 4)),
+            dma((3,)),
+            dma((3,)),
             dma((2, 8)),
             dma((2, 8)),
             dma((E,)),
@@ -546,7 +613,7 @@
             collective_id=0, has_side_effects=True, vmem_limit_bytes=62 * 1024 * 1024
         ),
         name="block",
-    )(mid, grad, block_in, qkv, gates, ids, w_in, w_out, w_qkv, w_proj, norm1, norm2)
+    )(mid, grad, block_in, qkv, routes, w_in, w_out, w_qkv, w_proj, norm1, norm2)
 
 
 def shards(
@@ -557,16 +624,15 @@
     count = window * window
     half = window // 2
 
-    def columns(a):
-        return a.reshape(2, half, 2, half, 2).transpose(0, 2, 1, 3, 4).reshape(count, 2)
-
+    routes = jnp.concatenate((gates, expert_ids.astype(F32)), -1)
+    routes = routes.reshape(2, half, 2, half, 4).transpose(0, 2, 1, 3, 4).reshape(count, 4)
+    routes = jnp.pad(routes, ((0, 0), (0, 124)))
     result = block(
         mid.reshape(count, width),
         grad_out.reshape(count, width),
         block_in.reshape(count, width),
         qkv.reshape(window, window, 3, width).transpose(0, 2, 1, 3),
-        columns(gates),
-        columns(expert_ids),
+        routes,
         w_in[0],
         w_out[0],
         w_qkv,

time: 226 us -> 200 us (0.88)
  Pallas kernels: 220 us -> 195 us
  local copies, waits for them, and re-layouts: 5.34 us -> 2.92 us
    pallas_call x1, Pallas kernels: 220 us -> 195 us  [block(): pl.pallas_call(block_kernel, out_shape=jax.ShapeDtypeStruct((256, 1024),...]
    reshape x4 -> x2, local copies, waits for them, and re-layouts: 3.45 us -> 0.37 us  [shards(): routes.reshape(2, half, 2, half, 4).transpose(0, 2, 1, 3, 4)]
where the time goes in v3:
time: 200 us; the launch traced here: 199 us
  Pallas kernels  195 us (98%)
  local copies, waits for them, and re-layouts  2.92 us (1%)
    pallas_call x1, Pallas kernels, block(): pl.pallas_call(block_kernel, out_shape=jax.ShapeDtypeStruct((256, 1024),...  195 us

profile of v3, /device:TPU:1, one launch (start us, length us, event | category | flops | bytes accessed | tf_op | source)
XLA Modules:
  0.0 199.2 jit_solution(6941322124973283349)
XLA Ops:
  0.0 0.7 convert_element_type.5
  0.7 0.7 pad_maximum_fusion
  1.5 0.1 reshape.31
  1.6 0.3 copy.13
  1.8 0.7 pad.4.routes_ref
  2.5 194.8 %block.1 = bf16[256,1024]{1,0:T(8,128)(2,1)} custom-call(bf16[256,1024]{1,0:T(8,128)(2,1)} %bitcast.20, bf16[256,1024]{1,0:T(8,128)(2,1)} %bitcast.21, bf16[256,1024]{1,0:T(8,128)(2,1)} %bitcast.22, bf16[16,3,16,1024]{3,2,1,0:T(8,128)(2,1)} %bitcast.19, f32[256,128]{1,0:T(8,128)} %pad.4.routes_ref, bf16[1024,1024]{1,0:T(8,128)(2,1)} %bitcast.16, ...), custom_call_target="tpu_custom_call" | custom-call | tf_op jit(solution)/shard_map/block/pallas_call | solution.py:576
  197.3 1.9 copy.15

commit v4 on v3

--- a/solution.py
+++ b/solution.py
@@ -94,6 +94,7 @@
     ret_in,
     choice,
     probs,
+    key_t,
     window_out,
     window_in,
     context_out,
@@ -191,8 +192,16 @@
             device_id_type=MESH,
         )
 
+    def cross(which, h):
+        return ship(which, source(which, h), 2 * z + h, h, place(x, y, h, w))
+
     for n in range(3):
         ship_tile(n).start()
+
+    @pl.when(outside)
+    def _():
+        for h in range(2):
+            cross(0, h).start()
 
     @pl.when(inside)
     def _():
@@ -204,8 +213,15 @@
                 ship(which, source(which, h), 2 * z + h, 2 + h, twin).start()
                 local(which, h).start()
 
-    def cross(which, h):
-        return ship(which, source(which, h), 2 * z + h, h, place(x, y, h, w))
+    def landed(which, piece):
+        pltpu.make_async_copy(
+            store[which].at[piece], store[which].at[piece], w_recv.at[which, piece]
+        ).wait()
+
+    def pass_on(which, piece, send_at, targets):
+        landed(which, piece)
+        for n, where in enumerate(targets):
+            ship(which, store[which].at[piece], piece, send_at + n, where).start()
 
     norm2 = norm2_ref[...]
 
@@ -301,62 +317,58 @@
         window_in[0, part] = rows[192:]
     for q in range(3):
         ship_quadrant(0, window_out, window_in, q, back[q]).start()
-    for n in range(3):
-        ship_tile(n).wait_send()
-
     @pl.when(outside)
     def _():
         for h in range(2):
-            cross(0, h).start()
-
+            cross(1, h).start()
+
+    for q in range(1, 4):
+        quadrant_landed(0, window_in, q)
+
+    last_row = (row == 7).astype(jnp.int32)
+    last_col = (col == 15).astype(jnp.int32)
+
+    def labels(shape, dim):
+        quadrant = lax.div(lax.broadcasted_iota(jnp.int32, shape, dim), 64)
+        return lax.div(quadrant, 2) * (2 * last_row) + lax.rem(quadrant, 2) * last_col
+
+    allowed = labels((256, 256), 0) == labels((256, 256), 1)
+    shut = jnp.where(allowed, 0.0, -1e30)
+    scale = 32**-0.5
+    head_of = lax.div(lax.broadcasted_iota(jnp.int32, (256, 128), 1), 32)
+    head_of_t = lax.div(lax.broadcasted_iota(jnp.int32, (128, 256), 0), 32)
+
+    def of_head(h, rows):
+        return jnp.where(head_of == h, rows, jnp.zeros_like(rows))
+
+    def stacked(rows):
+        return jnp.concatenate([of_head(h, rows) for h in range(4)], 0)
+
+    def window_part(part, lanes_at):
+        return window_in[:, part, :, lanes_at].reshape(256, 128)
+
+    def softmax_group(group, carry):
+        lanes_at = pl.ds(pl.multiple_of(group * 128, 128), 128)
+        query, key = window_part(0, lanes_at), window_part(1, lanes_at)
+        key_t[group] = jnp.transpose(key.astype(F32)).astype(BF16)
+        products = dot(stacked(key), query, (1, 1))
+        for h in range(4):
+            scores = products[256 * h : 256 * h + 256] * scale + shut
+            expo = jnp.exp(scores - jnp.max(scores, 0, keepdims=True))
+            prob = expo * (1.0 / jnp.sum(expo, 0, keepdims=True))
+            probs[group, :, 256 * h : 256 * h + 256] = prob.astype(BF16)
+        return carry
+
+    lax.fori_loop(0, HEADS // 4, softmax_group, 0)
+
+    onward = (place(x, y, c, u), twin)
+    pass_on(0, 2 * w + c, 4, onward)
     for n in range(3):
         pltpu.make_async_copy(tile[n][1], tile[n][1], m_recv.at[n]).wait()
     _, _, _, normed_m, sent_m, slots_m = prepare(
         mate_mid[...], mate_grad[...], mate_routes[...]
     )
     dispatch(normed_m, sent_m, slots_m, 1 - pair, mate)
-
-    for q in range(1, 4):
-        quadrant_landed(0, window_in, q)
-
-    last_row = (row == 7).astype(jnp.int32)
-    last_col = (col == 15).astype(jnp.int32)
-
-    def labels(shape, dim):
-        quadrant = lax.div(lax.broadcasted_iota(jnp.int32, shape, dim), 64)
-        return lax.div(quadrant, 2) * (2 * last_row) + lax.rem(quadrant, 2) * last_col
-
-    allowed = labels((256, 256), 0) == labels((256, 256), 1)
-    shut = jnp.where(allowed, 0.0, -1e30)
-    scale = 32**-0.5
-    head_of = lax.div(lax.broadcasted_iota(jnp.int32, (256, 128), 1), 32)
-
-    def of_head(h, rows):
-        return jnp.where(head_of == h, rows, jnp.zeros_like(rows))
-
-    def window_part(part, lanes_at):
-        return window_in[:, part, :, lanes_at].reshape(256, 128)
-
-    def softmax_group(group, carry):
-        lanes_at = pl.ds(pl.multiple_of(group * 128, 128), 128)
-        query, key = window_part(0, lanes_at), window_part(1, lanes_at)
-        for h in range(4):
-            scores = dot(of_head(h, key), query, (1, 1)) * scale + shut
-            expo = jnp.exp(scores - jnp.max(scores, 0, keepdims=True))
-            probs[4 * group + h] = (expo * (1.0 / jnp.sum(expo, 0, keepdims=True))).astype(BF16)
-        return carry
-
-    lax.fori_loop(0, HEADS // 4, softmax_group, 0)
-
-    def landed(which, piece):
-        pltpu.make_async_copy(
-            store[which].at[piece], store[which].at[piece], w_recv.at[which, piece]
-        ).wait()
-
-    def pass_on(which, piece, send_at, targets):
-        landed(which, piece)
-        for n, where in enumerate(targets):
-            ship(which, store[which].at[piece], piece, send_at + n, where).start()
 
     def product(piece, rows, begin):
         count = rows // C
@@ -377,14 +389,6 @@
 
         lax.fori_loop(0, 1024 // rows, one, 0)
 
-    @pl.when(outside)
-    def _():
-        for h in range(2):
-            cross(0, h).wait_send()
-            cross(1, h).start()
-
-    onward = (place(x, y, c, u), twin)
-    pass_on(0, 2 * w + c, 4, onward)
     for which in range(2):
         pass_on(which, 2 * u + c, 6, (twin,))
 
@@ -462,19 +466,17 @@
         ship(which, store[which].at[0], 0, send_at, twin).wait_send()
 
     for which in range(2):
-        for send_at in (4, 5, 6, 7):
+        for send_at in (0, 1, 4, 5, 6, 7):
             gone(which, send_at)
+
+    for n in range(3):
+        ship_tile(n).wait_send()
 
     @pl.when(inside)
     def _():
         for which in range(2):
-            for send_at in range(4):
+            for send_at in (2, 3):
                 gone(which, send_at)
-
-    @pl.when(outside)
-    def _():
-        for send_at in range(2):
-            gone(1, send_at)
 
     loads = [
         pltpu.make_async_copy(
@@ -494,8 +496,13 @@
         pltpu.make_async_copy(ret_in.at[m], ret_in.at[m], r_recv.at[m]).wait()
         return carry
 
-    lax.fori_loop(0, E, back_landed, 0)
-    normed_grad = dot(choice[...], ret_in[...].reshape(E * C, 1024))
+    normed_grad = jnp.zeros((256, 1024), F32)
+    for step in range(4):
+        block = lax.rem(y + 4 - step, 4)
+        lax.fori_loop(block * 8, block * 8 + 8, back_landed, 0)
+        picked = choice[:, pl.ds(pl.multiple_of(block * 256, 256), 256)]
+        rows = ret_in[pl.ds(block * 8, 8)].reshape(256, 1024)
+        normed_grad = normed_grad + dot(picked, rows)
     mid_grad = grad + norm_back(normed_grad, mid_hat, mid_inverse, norm2)
     mid_grad = mid_grad.astype(BF16)
 
@@ -515,20 +522,24 @@
     def heads_back(group, carry):
         begin = pl.multiple_of(group * 128, 128)
         lanes_at = pl.ds(begin, 128)
-        query, key, value = (window_part(part, lanes_at) for part in range(3))
+        query, _, value = (window_part(part, lanes_at) for part in range(3))
         out_grad = context_in[:, :, lanes_at].reshape(256, 128)
-        sums = [jnp.zeros((256, 128), F32)] * 3
+        products = dot(stacked(value), out_grad, (1, 1))
+        score_grads = []
         for h in range(4):
-            prob = probs[4 * group + h]
-            prob_f = prob.astype(F32)
-            prob_grad = dot(of_head(h, value), out_grad, (1, 1))
-            row_total = jnp.sum(prob_f * prob_grad, 0, keepdims=True)
-            score_grad = (prob_f * (prob_grad - row_total)).astype(BF16)
-            sums = [
-                sums[0] + dot(score_grad, of_head(h, key), (0, 0)),
-                sums[1] + dot(score_grad, of_head(h, query)),
-                sums[2] + dot(prob, of_head(h, out_grad)),
-            ]
+            prob = probs[group, :, 256 * h : 256 * h + 256].astype(F32)
+            prob_grad = products[256 * h : 256 * h + 256]
+            row_total = jnp.sum(prob * prob_grad, 0, keepdims=True)
+            score_grads.append((prob * (prob_grad - row_total)).astype(BF16))
+        turned = key_t[group]
+        turned = jnp.concatenate(
+            [jnp.where(head_of_t == h, turned, jnp.zeros_like(turned)) for h in range(4)], 1
+        )
+        sums = (
+            jnp.transpose(dot(turned, jnp.concatenate(score_grads, 0))),
+            dot(jnp.concatenate(score_grads, 1), stacked(query)),
+            dot(probs[group], stacked(out_grad)),
+        )
         for part, factor in enumerate((scale, scale, 1.0)):
             at = pl.ds(pl.multiple_of(part * 1024 + begin, 128), 128)
             heads_grad[:, at] = (sums[part] * factor).astype(BF16)
@@ -589,7 +600,8 @@
             pltpu.VMEM((E * C, 1024), F32),
             pltpu.VMEM((E, C, 1024), BF16),
             pltpu.VMEM((256, E * C), BF16),
-            pltpu.VMEM((HEADS, 256, 256), BF16),
+            pltpu.VMEM((HEADS // 4, 256, 1024), BF16),
+            pltpu.VMEM((HEADS // 4, 128, 256), BF16),
             pltpu.VMEM((4, 3, 64, 1024), BF16),
             pltpu.VMEM((4, 3, 64, 1024), BF16),
             pltpu.VMEM((4, 64, 1024), BF16),

time: 200 us -> 198 us (0.990)
  Pallas kernels: 195 us -> 191 us
    pallas_call x1, Pallas kernels: 195 us -> 191 us  [block(): pl.pallas_call(block_kernel, out_shape=jax.ShapeDtypeStruct((256, 1024),...]
where the time goes in v4:
time: 198 us; the launch traced here: 196 us
  Pallas kernels  191 us (96%)
  local copies, waits for them, and re-layouts  2.92 us (1%)
    pallas_call x1, Pallas kernels, block(): pl.pallas_call(block_kernel, out_shape=jax.ShapeDtypeStruct((256, 1024),...  191 us

profile of v4, /device:TPU:1, one launch (start us, length us, event | category | flops | bytes accessed | tf_op | source)
XLA Modules:
  0.0 195.7 jit_solution(15722782556381443469)
XLA Ops:
  0.0 0.7 convert_element_type.5
  0.7 0.7 pad_maximum_fusion
  1.5 0.1 reshape.31
  1.6 0.3 copy.13
  1.8 0.7 pad.4.routes_ref
  2.5 191.3 %block.1 = bf16[256,1024]{1,0:T(8,128)(2,1)} custom-call(bf16[256,1024]{1,0:T(8,128)(2,1)} %bitcast.20, bf16[256,1024]{1,0:T(8,128)(2,1)} %bitcast.21, bf16[256,1024]{1,0:T(8,128)(2,1)} %bitcast.22, bf16[16,3,16,1024]{3,2,1,0:T(8,128)(2,1)} %bitcast.19, f32[256,128]{1,0:T(8,128)} %pad.4.routes_ref, bf16[1024,1024]{1,0:T(8,128)(2,1)} %bitcast.16, ...), custom_call_target="tpu_custom_call" | custom-call | tf_op jit(solution)/shard_map/block/pallas_call | solution.py:587
  193.8 1.9 copy.15

commit v5 on v4

--- a/solution.py
+++ b/solution.py
@@ -317,11 +317,6 @@
         window_in[0, part] = rows[192:]
     for q in range(3):
         ship_quadrant(0, window_out, window_in, q, back[q]).start()
-    @pl.when(outside)
-    def _():
-        for h in range(2):
-            cross(1, h).start()
-
     for q in range(1, 4):
         quadrant_landed(0, window_in, q)
 
@@ -361,6 +356,11 @@
 
     lax.fori_loop(0, HEADS // 4, softmax_group, 0)
 
+    @pl.when(outside)
+    def _():
+        for h in range(2):
+            cross(1, h).start()
+
     onward = (place(x, y, c, u), twin)
     pass_on(0, 2 * w + c, 4, onward)
     for n in range(3):
@@ -391,6 +391,7 @@
 
     for which in range(2):
         pass_on(which, 2 * u + c, 6, (twin,))
+    pass_on(1, 2 * w + c, 4, onward)
 
     def rows_landed(m, carry):
         pltpu.make_async_copy(arrived.at[m], arrived.at[m], d_recv.at[m]).wait()
@@ -400,7 +401,6 @@
     for which in range(2):
         landed(which, 2 * z)
     whole(2 * z)
-    pass_on(1, 2 * w + c, 4, onward)
     for which in range(2):
         landed(which, 2 * z + 1)
     whole(2 * z + 1)

time: 198 us -> 196 us (0.990); the launches traced: 196 us -> 196 us
  no operation moved by 1% of the time
where the time goes in v5:
time: 196 us
  Pallas kernels  192 us (98%)
  local copies, waits for them, and re-layouts  2.92 us (1%)
    pallas_call x1, Pallas kernels, block(): pl.pallas_call(block_kernel, out_shape=jax.ShapeDtypeStruct((256, 1024),...  192 us

profile of v5, /device:TPU:1, one launch (start us, length us, event | category | flops | bytes accessed | tf_op | source)
XLA Modules:
  0.0 196.0 jit_solution(5171565770881023871)
XLA Ops:
  0.0 0.7 convert_element_type.5
  0.7 0.7 pad_maximum_fusion
  1.5 0.1 reshape.31
  1.6 0.3 copy.13
  1.8 0.7 pad.4.routes_ref
  2.5 191.6 %block.1 = bf16[256,1024]{1,0:T(8,128)(2,1)} custom-call(bf16[256,1024]{1,0:T(8,128)(2,1)} %bitcast.20, bf16[256,1024]{1,0:T(8,128)(2,1)} %bitcast.21, bf16[256,1024]{1,0:T(8,128)(2,1)} %bitcast.22, bf16[16,3,16,1024]{3,2,1,0:T(8,128)(2,1)} %bitcast.19, f32[256,128]{1,0:T(8,128)} %pad.4.routes_ref, bf16[1024,1024]{1,0:T(8,128)(2,1)} %bitcast.16, ...), custom_call_target="tpu_custom_call" | custom-call | tf_op jit(solution)/shard_map/block/pallas_call | solution.py:587
  194.1 1.9 copy.15

commit v6 on v5

--- a/solution.py
+++ b/solution.py
@@ -93,6 +93,7 @@
     total,
     ret_in,
     choice,
+    slopes,
     probs,
     key_t,
     window_out,
@@ -370,21 +371,33 @@
     )
     dispatch(normed_m, sent_m, slots_m, 1 - pair, mate)
 
-    def product(piece, rows, begin):
+    def product(piece, rows, begin, known=None):
         count = rows // C
         at = pl.ds(begin, count)
         normed_rows = arrived[at, 0].reshape(rows, 1024)
         grad_rows = arrived[at, 1].reshape(rows, 1024)
         first, second = w_first[piece], w_second[piece]
-        pre = dot(normed_rows, first)
+        if known is None:
+            slope = gelu_slope(dot(normed_rows, first))
+        else:
+            slope = slopes[known, pl.ds(pl.multiple_of(begin * C, 256), rows)]
         act_grad = dot(grad_rows, second, (1, 1))
-        pre_grad = (act_grad * gelu_slope(pre)).astype(BF16)
+        pre_grad = (act_grad * slope).astype(BF16)
         return dot(pre_grad, first, (1, 1))
 
-    def whole(piece, rows=512):
+    def slopes_of(known, piece):
+        def one(step, carry):
+            rows = arrived[pl.ds(step * 16, 16), 0].reshape(512, 1024)
+            at = pl.ds(pl.multiple_of(step * 512, 512), 512)
+            slopes[known, at] = gelu_slope(dot(rows, w_first[piece]))
+            return carry
+
+        lax.fori_loop(0, 2, one, 0)
+
+    def whole(piece, rows=512, known=None):
         def one(step, carry):
             at = pl.ds(pl.multiple_of(step * rows, rows), rows)
-            total[at] = total[at] + product(piece, rows, step * (rows // C))
+            total[at] = total[at] + product(piece, rows, step * (rows // C), known)
             return carry
 
         lax.fori_loop(0, 1024 // rows, one, 0)
@@ -413,10 +426,12 @@
     for which in range(2):
         landed(which, 2 * w + other)
     whole(2 * w + other)
+    slopes_of(0, 2 * v + c)
+    landed(0, 2 * v + other)
+    slopes_of(1, 2 * v + other)
     pass_on(1, 2 * v + c, 7, (twin,))
-    whole(2 * v + c)
-    for which in range(2):
-        landed(which, 2 * v + other)
+    whole(2 * v + c, known=0)
+    landed(1, 2 * v + other)
 
     def rows_gone(at, carry):
         @pl.when((at != me) & (at != mate))
@@ -440,7 +455,7 @@
     def last(step, carry):
         block = lax.rem(y + step, 4)
         at = pl.ds(pl.multiple_of(block * 256, 256), 256)
-        done = total[at] + product(2 * v + other, 256, block * 8)
+        done = total[at] + product(2 * v + other, 256, block * 8, 1)
         outgoing[pl.ds(block * 8, 8), 0] = done.astype(BF16).reshape(8, C, 1024)
 
         def send_one(k, carry):
@@ -600,6 +615,7 @@
             pltpu.VMEM((E * C, 1024), F32),
             pltpu.VMEM((E, C, 1024), BF16),
             pltpu.VMEM((256, E * C), BF16),
+            pltpu.VMEM((2, E * C, HID), F32),
             pltpu.VMEM((HEADS // 4, 256, 1024), BF16),
             pltpu.VMEM((HEADS // 4, 128, 256), BF16),
             pltpu.VMEM((4, 3, 64, 1024), BF16),

time: 196 us -> 202 us (1.031)
  Pallas kernels: 192 us -> 196 us
    pallas_call x1, Pallas kernels: 192 us -> 196 us  [block(): pl.pallas_call(block_kernel, out_shape=jax.ShapeDtypeStruct((256, 1024),...]
where the time goes in v6:
time: 202 us; the launch traced here: 201 us
  Pallas kernels  196 us (97%)
  local copies, waits for them, and re-layouts  2.92 us (1%)
    pallas_call x1, Pallas kernels, block(): pl.pallas_call(block_kernel, out_shape=jax.ShapeDtypeStruct((256, 1024),...  196 us

profile of v6, /device:TPU:1, one launch (start us, length us, event | category | flops | bytes accessed | tf_op | source)
XLA Modules:
  0.0 200.6 jit_solution(10199996225499026039)
XLA Ops:
  0.0 0.7 convert_element_type.5
  0.7 0.7 pad_maximum_fusion
  1.5 0.1 reshape.31
  1.6 0.3 copy.13
  1.8 0.7 pad.4.routes_ref
  2.5 196.2 %block.1 = bf16[256,1024]{1,0:T(8,128)(2,1)} custom-call(bf16[256,1024]{1,0:T(8,128)(2,1)} %bitcast.20, bf16[256,1024]{1,0:T(8,128)(2,1)} %bitcast.21, bf16[256,1024]{1,0:T(8,128)(2,1)} %bitcast.22, bf16[16,3,16,1024]{3,2,1,0:T(8,128)(2,1)} %bitcast.19, f32[256,128]{1,0:T(8,128)} %pad.4.routes_ref, bf16[1024,1024]{1,0:T(8,128)(2,1)} %bitcast.16, ...), custom_call_target="tpu_custom_call" | custom-call | tf_op jit(solution)/shard_map/block/pallas_call | solution.py:602
  198.7 1.9 copy.15
